TPU v7x, 256 devices: a whole 4x4x8 slice. The times are simulated.
256 devices in a mesh: lon: 32 (over z, y_lo, core), lat: 8 (over y_hi, x).
Axes of the slice: x: 4, y: 4 (y_hi: 2, y_lo: 2; y = y_hi * 2 + y_lo), z: 8, core: 2. Of those that a mesh axis runs over, the one named last changes fastest.
Arguments:
- patches: bfloat16 [64, 1024, 1104], P('lat', 'lon'), may hold values from -6 to 6
- embed_weight: bfloat16 [1104, 768], replicated, may hold values from -0.1875 to 0.1875
- embed_bias: float32 [768], replicated, may hold values from -3 to 3
- conv_weight: bfloat16 [3, 3, 768, 768], P(None, None, None, 'lat'), may hold values from -0.078125 to 0.078125
- conv_bias: float32 [768], replicated, may hold values from -3 to 3
- norm_gain: float32 [768], replicated, may hold values from 0.1 to 1.9
- up_weight: bfloat16 [768, 3072], P(None, 'lon'), may hold values from -0.21875 to 0.21875
- up_bias: float32 [1, 3072], P(None, 'lon'), may hold values from -3 to 3
- down_weight: bfloat16 [768, 3072], P(None, 'lon'), may hold values from -0.109375 to 0.109375
- down_bias: float32 [768], replicated, may hold values from -3 to 3
Outputs:
- features: bfloat16 [64, 1024, 768], P('lat', 'lon')
All inputs are finite; a program needn't handle non-finite values.
Results may differ from a plain program's by a relative error of at most 0.022.
Values may be sent and summed in bfloat16 or wider, within the bound.
A program may use at most 128 MiB of HBM per device.

v0:
```python
import jax
import jax.numpy as jnp
from jax import lax
from jax.sharding import PartitionSpec as P


def extended(value, sides, width, wrap):
    for axis, dim in sides:
        size, length = (lax.axis_size(axis), value.shape[dim])
        up = [(i, (i + 1) % size) for i in range(size if wrap else size - 1)]
        down = [(j, i) for i, j in up]
        last = lax.slice_in_dim(value, length - width, length, axis=dim)
        leading = lax.slice_in_dim(value, 0, width, axis=dim)
        before = lax.ppermute(last, axis, up)
        after = lax.ppermute(leading, axis, down)
        value = jnp.concatenate([before, value, after], axis=dim)
    return value


def stencil(framed, kernel, rows, cols, width):
    total = jnp.zeros((rows * cols, kernel.shape[3]), jnp.float32)
    for row_off in range(3):
        for col_off in range(3):
            window = framed[row_off : row_off + rows, col_off : col_off + cols].reshape(
                rows * cols, width
            )
            total = total + jnp.dot(
                window, kernel[row_off, col_off], preferred_element_type=jnp.float32
            )
    return total.reshape(rows, cols, kernel.shape[3])


def body(
    patches,
    embed_weight,
    embed_bias,
    conv_weight,
    conv_bias,
    norm_gain,
    up_weight,
    up_bias,
    down_weight,
    down_bias,
):
    rows, cols, inputs = patches.shape
    width = embed_weight.shape[1]
    embedded = (
        jnp.dot(
            patches.reshape(rows * cols, inputs), embed_weight, preferred_element_type=jnp.float32
        )
        + embed_bias
    ).astype(jnp.bfloat16)
    embedded = embedded.reshape(rows, cols, width)
    activated = jax.nn.gelu(embedded.astype(jnp.float32)).astype(jnp.bfloat16)
    widened = extended(activated, (("lon", 1),), 1, True)
    framed = extended(widened, (("lat", 0),), 1, False)
    convolved = stencil(
        framed, lax.all_gather(conv_weight, "lat", axis=3, tiled=True), rows, cols, width
    )
    mixed = (embedded.astype(jnp.float32) + convolved + conv_bias).astype(jnp.bfloat16)
    values = mixed.astype(jnp.float32)
    center = jnp.mean(values, axis=2, keepdims=True)
    spread = jnp.mean((values - center) ** 2, axis=2, keepdims=True)
    normed = ((values - center) * lax.rsqrt(spread + 1e-05) * norm_gain).astype(jnp.bfloat16)
    piece = lax.all_gather(normed, "lon", axis=1, tiled=True)
    count = piece.shape[1]
    flat_tokens = piece.reshape(rows * count, width)
    hidden = jax.nn.gelu(
        jnp.dot(flat_tokens, up_weight, preferred_element_type=jnp.float32) + up_bias
    ).astype(jnp.bfloat16)
    result = lax.dot_general(
        hidden, down_weight, (((1,), (1,)), ((), ())), preferred_element_type=jnp.float32
    )
    terms = result.reshape(rows, count, width)
    summed = lax.psum_scatter(
        terms.astype(jnp.bfloat16), "lon", scatter_dimension=1, tiled=True
    ).astype(jnp.float32)
    return (values + summed + down_bias).astype(jnp.bfloat16)


def solution(mesh):
    in_specs = (
        P("lat", "lon", None),
        P(),
        P(),
        P(None, None, None, "lat"),
        P(),
        P(),
        P(None, "lon"),
        P(None, "lon"),
        P(None, "lon"),
        P(),
    )
    out_specs = P("lat", "lon", None)
    return jax.shard_map(body, mesh=mesh, in_specs=in_specs, out_specs=out_specs, check_vma=False)
```

profile of v0, /device:TPU:1, one launch (start us, length us, event | category | flops | bytes accessed | tf_op | source)
XLA Modules:
  0.0 410.2 jit_solution(4687578264278024501)
XLA Ops:
  6.5 0.7 all-gather.3.cloned.1.call-update
  7.3 0.7 copy-done
  8.0 1.7 fusion.16
  10.0 2.8 collective-permute-start
  12.8 0.6 collective-permute-start.1
  13.4 0.6 collective-permute-done
  14.1 2.0 collective-permute-done.1
  16.1 3.1 collective-permute-start.2
  19.2 1.3 collective-permute-start.3
  20.5 1.1 pad_maximum_fusion.1
  21.6 2.6 collective-permute-done.3
  24.4 1.5 fusion.56
  25.9 121.9 %all-gather.3.cloned.1.call-done = bf16[3,3,768,768]{2,3,1,0:T(8,128)(2,1)} async-done(((bf16[3,3,768,96]{2,3,1,0:T(8,128)(2,1)}), bf16[3,3,768,768]{2,3,1,0:T(8,128)(2,1)}) %all-gather.3.cloned.1.call-update) | async-done | bytes 10616848 | tf_op jit(solution)/shard_map/all_gather | solution.py:58
  147.9 2.0 fusion.18
  149.9 2.4 fusion.17
  152.2 1.9 fusion.19
  154.2 2.0 convolution_add_fusion.6
  158.3 1.3 convert_reduce_fusion
  159.7 1.2 fusion.26
  161.0 1.1 fusion.22
  162.2 78.9 %all-gather.5.cloned.1.call-done = bf16[8,1024,768]{2,1,0:T(8,128)(2,1)} async-done(((bf16[8,32,768]{2,1,0:T(8,128)(2,1)}), bf16[8,1024,768]{2,1,0:T(8,128)(2,1)}) %all-gather.5.cloned.1.call-update) | async-done | bytes 12582928 | tf_op jit(solution)/shard_map/all_gather | solution.py:65
  241.1 12.9 %convolution_convert_fusion = bf16[8192,768]{1,0:T(8,128)(2,1)} fusion(bf16[768,96]{0,1:T(8,128)(2,1)} %param.18, bf16[8192,768]{1,0:T(8,128)(2,1)} %bitcast.57, bf16[768,96]{0,1:T(8,128)(2,1)S(1)} %copy-done.6, f32[96]{0:T(128)S(1)} %bitcast.69), kind=kOutput, calls=%fused_computation | convolution fusion | flops 2430074880 | bytes 25461120 | tf_op jit(solution)/shard_map/dot_general | solution.py:71
  254.0 147.8 %reduce-scatter.2.cloned.1.call-done = bf16[8,32,768]{2,1,0:T(8,128)(2,1)} async-done(((bf16[8,1024,768]{2,1,0:T(8,128)(2,1)}), bf16[8,32,768]{2,1,0:T(8,128)(2,1)}) %reduce-scatter.2.cloned.1.call-update) | async-done | bytes 393232 | tf_op jit(solution)/shard_map/reduce_scatter | solution.py:75
  401.8 1.9 fusion.24
  (39 shorter events, 3.0 us)
Async XLA Ops:
  6.5 1.5 copy-start
  6.5 141.3 %all-gather.3.cloned.1.call-start = ((), (), s32[]{:S(2)}) async-start(), calls=%async_computation.1 | async-start | bytes 11943936 | tf_op jit(solution)/shard_map/all_gather | solution.py:58
  7.3 233.9 %all-gather.5.cloned.1.call-start = ((), (), s32[]{:S(2)}) async-start(), calls=%async_computation.2 | async-start | bytes 12976128 | tf_op jit(solution)/shard_map/all_gather | solution.py:65
  10.0 4.0 collective-permute-start
  12.8 3.3 collective-permute-start.1
  16.1 5.5 %collective-permute-start.2 = (bf16[1,34,768]{2,1,0:T(8,128)(2,1)S(1)}, bf16[1,34,768]{2,1,0:T(8,128)(2,1)S(1)}, u32[]{:S(2)}, u32[]{:S(2)}) collective-permute-start(bf16[1,34,768]{2,1,0:T(8,128)(2,1)S(1)} %get-tuple-element.17), channel_id=1, source_target_pairs={{0,1},{1,2},{2,3},{3,4},{4,5},{5,6},{6,7},{8,9},{9,10},{10,11},{11... | collective-permute-start | bytes 156680 | tf_op jit(solution)/shard_map/ppermute | solution.py:14
  19.2 5.0 %collective-permute-start.3 = (bf16[1,34,768]{2,1,0:T(8,128)(2,1)S(1)}, bf16[1,34,768]{2,1,0:T(8,128)(2,1)S(1)}, u32[]{:S(2)}, u32[]{:S(2)}) collective-permute-start(bf16[1,34,768]{2,1,0:T(8,128)(2,1)S(1)} %get-tuple-element.18), channel_id=1, source_target_pairs={{1,0},{2,1},{3,2},{4,3},{5,4},{6,5},{7,6},{9,8},{10,9},{11,10},{12... | collective-permute-start | bytes 156680 | tf_op jit(solution)/shard_map/ppermute | solution.py:15
  147.9 8.3 %copy-start.1 = (bf16[3,3,768,768]{2,3,1,0:T(8,128)(2,1)S(1)}, bf16[3,3,768,768]{2,3,1,0:T(8,128)(2,1)}, u32[]{:S(2)}) copy-start(bf16[3,3,768,768]{2,3,1,0:T(8,128)(2,1)} %all-gather.3.cloned.1.call-done) | copy-start | bytes 31850500
  154.1 2.5 copy-start.5
  156.1 1.1 copy-start.4
  157.2 1.1 copy-start.3
  157.2 1.1 copy-start.7
  158.3 2.8 copy-start.8
  158.3 82.8 %copy-start.6 = (bf16[768,96]{0,1:T(8,128)(2,1)S(1)}, bf16[768,96]{0,1:T(8,128)(2,1)}, u32[]{:S(2)}) copy-start(bf16[768,96]{0,1:T(8,128)(2,1)} %param.16) | copy-start | bytes 442372
  158.3 82.8 %copy-start.10 = (f32[1,96]{1,0:T(1,128)S(1)}, f32[1,96]{1,0:T(1,128)}, u32[]{:S(2)}) copy-start(f32[1,96]{1,0:T(1,128)} %param.17) | copy-start | bytes 1156
  162.1 239.7 %reduce-scatter.2.cloned.1.call-start = ((), (), s32[]{:S(2)}) async-start(), calls=%async_computation.3 | async-start | bytes 12976128 | tf_op jit(solution)/shard_map/reduce_scatter | solution.py:75
  254.0 147.8 %copy-start.2 = (bf16[8,32,768]{2,1,0:T(8,128)(2,1)S(1)}, bf16[8,32,768]{2,1,0:T(8,128)(2,1)}, u32[]{:S(2)}) copy-start(bf16[8,32,768]{2,1,0:T(8,128)(2,1)} %get-tuple-element.6) | copy-start | bytes 1179652
  254.0 147.8 %copy-start.9 = (f32[768]{0:T(1024)S(1)}, f32[768]{0:T(1024)}, u32[]{:S(2)}) copy-start(f32[768]{0:T(1024)} %param.19) | copy-start | bytes 9220
Sparse Core Ops, SparseCore 0:
  9.9 137.9 all-gather.2
  162.3 78.7 all-gather.4
  254.1 147.6 reduce-scatter.1
where the time goes:
time: 414 us; the launch traced here: 410 us
  waiting for transfers between devices  355 us (86%)
  matrix products  26.2 us (6%)
  between operations  13.3 us (3%)
  starting transfers between devices  7.9 us (2%)
  other arithmetic  5.87 us (1%)
    reduce_scatter x1, waiting for transfers between devices, body(): lax.psum_scatter(terms.astype(jnp.bfloat16), 'lon', scatter_dimension=1,...  148 us
    all_gather x1, waiting for transfers between devices, body(): lax.all_gather(conv_weight, 'lat', axis=3, tiled=True)  122 us
    all_gather x1, waiting for transfers between devices, body(): piece = lax.all_gather(normed, 'lon', axis=1, tiled=True)  78.9 us
    dot_general x1, matrix products, body(): lax.dot_general(hidden, down_weight, (((1,), (1,)), ((), ())), preferred_...  12.9 us
    dot_general x9, matrix products, stencil(): jnp.dot(window, kernel[row_off, col_off], preferred_element_type=jnp.floa...  11.6 us
  transfers between devices with their start and end apart: 7, of which 6 were waited for; matrix products, arithmetic and copies ran while one was open for 1% of the time, Pallas kernels for 0%

commit v1 on v0

--- a/solution.py
+++ b/solution.py
@@ -62,20 +62,18 @@
     center = jnp.mean(values, axis=2, keepdims=True)
     spread = jnp.mean((values - center) ** 2, axis=2, keepdims=True)
     normed = ((values - center) * lax.rsqrt(spread + 1e-05) * norm_gain).astype(jnp.bfloat16)
-    piece = lax.all_gather(normed, "lon", axis=1, tiled=True)
-    count = piece.shape[1]
-    flat_tokens = piece.reshape(rows * count, width)
+    up_all = lax.all_gather(up_weight.T, "lon", axis=0, tiled=True)
+    bias_all = lax.all_gather(up_bias, "lon", axis=1, tiled=True)
+    down_all = lax.all_gather(down_weight.T, "lon", axis=0, tiled=True)
+    flat_tokens = normed.reshape(rows * cols, width)
     hidden = jax.nn.gelu(
-        jnp.dot(flat_tokens, up_weight, preferred_element_type=jnp.float32) + up_bias
+        lax.dot_general(
+            flat_tokens, up_all, (((1,), (1,)), ((), ())), preferred_element_type=jnp.float32
+        )
+        + bias_all
     ).astype(jnp.bfloat16)
-    result = lax.dot_general(
-        hidden, down_weight, (((1,), (1,)), ((), ())), preferred_element_type=jnp.float32
-    )
-    terms = result.reshape(rows, count, width)
-    summed = lax.psum_scatter(
-        terms.astype(jnp.bfloat16), "lon", scatter_dimension=1, tiled=True
-    ).astype(jnp.float32)
-    return (values + summed + down_bias).astype(jnp.bfloat16)
+    result = jnp.dot(hidden, down_all, preferred_element_type=jnp.float32)
+    return (values + result.reshape(rows, cols, width) + down_bias).astype(jnp.bfloat16)
 
 
 def solution(mesh):

time: 414 us -> 305 us (0.74)
  waiting for transfers between devices: 355 us -> 148 us
  blocking collectives: 0 us -> 107 us
  matrix products: 26.2 us -> 20.4 us
    reduce_scatter x1 -> x0, waiting for transfers between devices: 148 us -> none  [body(): lax.psum_scatter(terms.astype(jnp.bfloat16), 'lon', scatter_dimension=1,...]
    unnamed x0 -> x1, blocking collectives: none -> 107 us
    all_gather x1, waiting for transfers between devices: 122 us -> 16.9 us  [body(): lax.all_gather(conv_weight, 'lat', axis=3, tiled=True)]
    all_gather x1 -> x2, waiting for transfers between devices: 78.9 us -> 125 us  [the longest x1 69.4 us: body(): down_all = lax.all_gather(down_weight.T, 'lon', axis=0, tiled=True)]
    dot_general x1, matrix products: 12.9 us -> 7.64 us  [body(): result = jnp.dot(hidden, down_all, preferred_element_type=jnp.float32)]
  transfers between devices with their start and end apart: 7 -> 7, of which waited for: 6 -> 4; matrix products, arithmetic and copies ran while one was open for 1% -> 6% of each run, Pallas kernels for 0% -> 0%
where the time goes in v1:
time: 305 us
  waiting for transfers between devices  148 us (49%)
  blocking collectives  107 us (35%)
  matrix products  20.4 us (7%)
  between operations  14 us (5%)
  starting transfers between devices  7.86 us (3%)
  other arithmetic  4.01 us (1%)
    unnamed x1, blocking collectives  107 us
    all_gather x1, waiting for transfers between devices, body(): down_all = lax.all_gather(down_weight.T, 'lon', axis=0, tiled=True)  69.4 us
    all_gather x1, waiting for transfers between devices, body(): up_all = lax.all_gather(up_weight.T, 'lon', axis=0, tiled=True)  55.9 us
    all_gather x1, waiting for transfers between devices, body(): lax.all_gather(conv_weight, 'lat', axis=3, tiled=True)  16.9 us
    dot_general x9, matrix products, stencil(): jnp.dot(window, kernel[row_off, col_off], preferred_element_type=jnp.floa...  11.1 us
    dot_general x1, matrix products, body(): result = jnp.dot(hidden, down_all, preferred_element_type=jnp.float32)  7.64 us
  transfers between devices with their start and end apart: 7, of which 4 were waited for; matrix products, arithmetic and copies ran while one was open for 6% of the time, Pallas kernels for 0%

profile of v1, /device:TPU:1, one launch (start us, length us, event | category | flops | bytes accessed | tf_op | source)
XLA Modules:
  0.0 304.7 jit_solution(5475071710373852603)
XLA Ops:
  6.5 0.7 all-gather.4.cloned.1.call-update
  7.3 0.7 all-gather.6.cloned.1.call-update
  8.1 0.7 all-gather.8.cloned.1.call-update
  8.8 1.7 fusion.11
  10.8 2.8 collective-permute-start
  13.6 0.6 collective-permute-start.1
  14.2 0.6 dynamic-slice
  15.6 107.3 %all-reduce = f32[3072]{0:T(1024)S(1)} all-reduce(f32[3072]{0:T(1024)S(1)} %bitcast_dynamic-update-slice_fusion), channel_id=1, replica_groups=mesh['lon'=32,'lat'=8] {'lon'}, use_global_device_ids=true, to_apply=%add | all-reduce | flops 3072 | bytes 24576
  123.0 3.1 %collective-permute-start.2 = (bf16[1,34,768]{2,1,0:T(8,128)(2,1)S(1)}, bf16[1,34,768]{2,1,0:T(8,128)(2,1)S(1)}, u32[]{:S(2)}, u32[]{:S(2)}) collective-permute-start(bf16[1,34,768]{2,1,0:T(8,128)(2,1)S(1)} %get-tuple-element.15), channel_id=1, source_target_pairs={{0,1},{1,2},{2,3},{3,4},{4,5},{5,6},{6,7},{8,9},{9,10},{10,11},{11... | collective-permute-start | bytes 156680 | tf_op jit(solution)/shard_map/ppermute | solution.py:14
  126.1 1.3 collective-permute-start.3
  127.4 1.1 pad_maximum_fusion.1
  128.5 3.8 %collective-permute-done.3 = bf16[1,34,768]{2,1,0:T(8,128)(2,1)S(1)} collective-permute-done((bf16[1,34,768]{2,1,0:T(8,128)(2,1)S(1)}, bf16[1,34,768]{2,1,0:T(8,128)(2,1)S(1)}, u32[]{:S(2)}, u32[]{:S(2)}) %collective-permute-start.3) | collective-permute-done | bytes 52256 | tf_op jit(solution)/shard_map/ppermute | solution.py:15
  132.5 1.4 fusion.58
  134.0 16.9 %all-gather.4.cloned.1.call-done = bf16[3,3,768,768]{2,3,1,0:T(8,128)(2,1)} async-done(((bf16[3,3,768,96]{2,3,1,0:T(8,128)(2,1)}), bf16[3,3,768,768]{2,3,1,0:T(8,128)(2,1)}) %all-gather.4.cloned.1.call-update) | async-done | bytes 10616848 | tf_op jit(solution)/shard_map/all_gather | solution.py:58
  150.9 2.0 fusion.14
  152.9 2.6 fusion.12
  155.6 1.9 fusion.13
  157.5 1.8 convolution_add_fusion.6
  161.5 0.6 convert_reduce_fusion
  162.1 0.7 copy-done.4
  163.1 55.9 %all-gather.6.cloned.1.call-done = bf16[3072,768]{1,0:T(8,128)(2,1)} async-done(((bf16[96,768]{1,0:T(8,128)(2,1)}), bf16[3072,768]{1,0:T(8,128)(2,1)}) %all-gather.6.cloned.1.call-update) | async-done | bytes 4718608 | tf_op jit(solution)/shard_map/all_gather | solution.py:65
  219.0 69.4 %all-gather.8.cloned.1.call-done = bf16[3072,768]{1,0:T(8,128)(2,1)} async-done(((bf16[96,768]{1,0:T(8,128)(2,1)}), bf16[3072,768]{1,0:T(8,128)(2,1)}) %all-gather.8.cloned.1.call-update) | async-done | bytes 4718608 | tf_op jit(solution)/shard_map/all_gather | solution.py:67
  288.4 7.6 %fusion.36 = f32[256,768]{1,0:T(8,128)} fusion(bf16[3072,768]{1,0:T(8,128)(2,1)} %all-gather.8.cloned.1.call-done, bf16[3072,768]{1,0:T(8,128)(2,1)} %all-gather.6.cloned.1.call-done, f32[3072]{0:T(1024)S(1)} %all-reduce, bf16[256,768]{1,0:T(8,128)(2,1)} %copy-done.4, f32[768]{0:T(1024)S(1)} %copy-done.9, f32[256]{0:T(256)S(1)} %add_rsqrt_fusion, ...), kind=kOutput, calls=%fused_computation.61 | convolution fusion | flops 2424766464 | bytes 10634240 | tf_op jit(solution)/shard_map/dot_general | solution.py:75
  296.0 2.1 add_convert_fusion
  (42 shorter events, 3.1 us)
Async XLA Ops:
  6.5 2.2 copy-start
  6.5 7.7 %copy-start.11 = (u32[256]{0:T(256)S(1)}, u32[256]{0:T(256)}, u32[]{:S(2)}) copy-start(u32[256]{0:T(256)} %constant.22) | copy-start | bytes 3076
  6.5 8.9 %copy-start.10 = (f32[1,96]{1,0:T(1,128)S(1)}, f32[1,96]{1,0:T(1,128)}, u32[]{:S(2)}) copy-start(f32[1,96]{1,0:T(1,128)} %param.17) | copy-start | bytes 1156
  6.5 144.3 %all-gather.4.cloned.1.call-start = ((), (), s32[]{:S(2)}) async-start(), calls=%async_computation | async-start | bytes 11943936 | tf_op jit(solution)/shard_map/all_gather | solution.py:58
  7.3 211.7 %all-gather.6.cloned.1.call-start = ((), (), s32[]{:S(2)}) async-start(), calls=%async_computation.1 | async-start | bytes 4866048 | tf_op jit(solution)/shard_map/all_gather | solution.py:65
  8.0 280.3 %all-gather.8.cloned.1.call-start = ((), (), s32[]{:S(2)}) async-start(), calls=%async_computation.2 | async-start | bytes 4866048 | tf_op jit(solution)/shard_map/all_gather | solution.py:67
  10.8 112.1 %collective-permute-start = (bf16[8,1,768]{2,1,0:T(2,128)(2,1)S(1)}, bf16[8,1,768]{2,1,0:T(2,128)(2,1)S(1)}, u32[]{:S(2)}, u32[]{:S(2)}) collective-permute-start(bf16[8,1,768]{2,1,0:T(2,128)(2,1)S(1)} %get-tuple-element.19), channel_id=1, source_target_pairs={{0,8},{8,16},{16,24},{24,32},{32,40},{40,48},{48,56},{56,64},{64,7... | collective-permute-start | bytes 36872 | tf_op jit(solution)/shard_map/ppermute | solution.py:14
  13.6 109.4 %collective-permute-start.1 = (bf16[8,1,768]{2,1,0:T(2,128)(2,1)S(1)}, bf16[8,1,768]{2,1,0:T(2,128)(2,1)S(1)}, u32[]{:S(2)}, u32[]{:S(2)}) collective-permute-start(bf16[8,1,768]{2,1,0:T(2,128)(2,1)S(1)} %get-tuple-element.20), channel_id=1, source_target_pairs={{8,0},{16,8},{24,16},{32,24},{40,32},{48,40},{56,48},{64,56},{72,6... | collective-permute-start | bytes 36872 | tf_op jit(solution)/shard_map/ppermute | solution.py:15
  123.0 5.5 %collective-permute-start.2 = (bf16[1,34,768]{2,1,0:T(8,128)(2,1)S(1)}, bf16[1,34,768]{2,1,0:T(8,128)(2,1)S(1)}, u32[]{:S(2)}, u32[]{:S(2)}) collective-permute-start(bf16[1,34,768]{2,1,0:T(8,128)(2,1)S(1)} %get-tuple-element.15), channel_id=1, source_target_pairs={{0,1},{1,2},{2,3},{3,4},{4,5},{5,6},{6,7},{8,9},{9,10},{10,11},{11... | collective-permute-start | bytes 156680 | tf_op jit(solution)/shard_map/ppermute | solution.py:14
  126.1 6.2 %collective-permute-start.3 = (bf16[1,34,768]{2,1,0:T(8,128)(2,1)S(1)}, bf16[1,34,768]{2,1,0:T(8,128)(2,1)S(1)}, u32[]{:S(2)}, u32[]{:S(2)}) collective-permute-start(bf16[1,34,768]{2,1,0:T(8,128)(2,1)S(1)} %get-tuple-element.16), channel_id=1, source_target_pairs={{1,0},{2,1},{3,2},{4,3},{5,4},{6,5},{7,6},{9,8},{10,9},{11,10},{12... | collective-permute-start | bytes 156680 | tf_op jit(solution)/shard_map/ppermute | solution.py:15
  150.9 6.6 %copy-start.2 = (bf16[8,32,768]{2,1,0:T(8,128)(2,1)S(1)}, bf16[8,32,768]{2,1,0:T(8,128)(2,1)}, u32[]{:S(2)}) copy-start(bf16[8,32,768]{2,1,0:T(8,128)(2,1)} %get-tuple-element.22) | copy-start | bytes 1179652
  150.9 8.4 %copy-start.1 = (bf16[3,3,768,768]{2,3,1,0:T(8,128)(2,1)S(1)}, bf16[3,3,768,768]{2,3,1,0:T(8,128)(2,1)}, u32[]{:S(2)}) copy-start(bf16[3,3,768,768]{2,3,1,0:T(8,128)(2,1)} %all-gather.4.cloned.1.call-done) | copy-start | bytes 31850500
  157.5 2.4 copy-start.6
  159.3 1.1 copy-start.5
  160.4 1.1 copy-start.3
  160.4 1.1 copy-start.7
  161.4 126.9 %copy-start.9 = (f32[768]{0:T(1024)S(1)}, f32[768]{0:T(1024)}, u32[]{:S(2)}) copy-start(f32[768]{0:T(1024)} %param.15) | copy-start | bytes 9220
  162.1 0.8 copy-start.4
  163.1 132.9 %copy-start.8 = (f32[768]{0:T(1024)S(1)}, f32[768]{0:T(1024)}, u32[]{:S(2)}) copy-start(f32[768]{0:T(1024)} %param.19) | copy-start | bytes 9220
Sparse Core Ops, SparseCore 0:
  9.9 140.9 all-gather.3
  152.7 66.2 all-gather.5
  220.9 67.4 all-gather.7

commit v2 on v1

v2 whole, which is shorter than its diff:
```python
import functools

import jax
import jax.numpy as jnp
from jax import lax
from jax.experimental import pallas as pl
from jax.experimental.pallas import tpu as pltpu
from jax.sharding import PartitionSpec as P

MESH = pl.DeviceIdType.MESH
NX, NZ = 4, 8
ROWS, COLS, WIDTH, UNITS = 8, 32, 768, 96
TOKENS, HALF, TILE = ROWS * COLS, UNITS // 2, 256
TAPS = 9
Y_FIRST = (0, 0, 1, 1, 1, 0, 0, 1, 1)
WAY = (-1, -1, 1, -1, 1, 1, -1, -1, 1)
ORDER = (
    ("own", 0), ("own", 1), ("own", 2), ("own", 3), ("own", 4), ("mlp",), ("embed",), ("near", 0), ("near", 1), ("own", 5),
    ("own", 6), ("mlp_y",), ("across", 2), ("share_up", 0), ("across", 3), ("own", 7), ("share_down", 0), ("across", 4), ("down", 1, "p"),
    ("down", 1, "m"), ("far", 0), ("own", 8), ("up", 1, "p"), ("up", 1, "m"), ("far", 1), ("share_up", 1, "p"), ("share_up", 1, "m"),
    ("share_down", 1, "p"), ("near", 5), ("down", 2, "p"), ("down", 2, "m"), ("near", 6), ("share_down", 1, "m"), ("near", 2), ("near", 3),
    ("across", 7), ("share_down", 2, "p"), ("share", 0), ("up", 2, "p"), ("up", 2, "m"), ("near", 4), ("far", 5), ("share_up", 2, "p"),
    ("share_up", 2, "m"), ("across", 8), ("share_down", 2, "m"), ("conv", 0), ("share", 1), ("down", 3, "p"), ("down", 3, "m"), ("far", 2),
    ("far", 6), ("share", 2), ("conv", 1), ("conv", 2), ("far", 3), ("share", 3), ("share_down", 3, "p"), ("near", 7), ("far", 4),
    ("share", 4), ("conv", 3), ("up", 3, "p"), ("up", 3, "m"), ("near", 8), ("share_up", 3, "p"), ("share_up", 3, "m"), ("conv", 4),
    ("share", 5), ("down", 4, "p"), ("down", 4, "m"), ("share_down", 3, "m"), ("down_far",), ("share", 6), ("far", 7), ("share", 7), ("conv", 5),
    ("up", 4, "p"), ("up", 4, "m"), ("far", 8), ("share", 8), ("share_up", 4), ("conv", 6), ("conv", 7), ("share_down", 4), ("conv", 8),
)


def gelu(v):
    return 0.5 * v * (1.0 + jnp.tanh(0.7978845608028654 * (v + 0.044715 * (v * v * v))))


def nt(a, b):
    return lax.dot_general(a, b, (((1,), (1,)), ((), ())), preferred_element_type=jnp.float32)


class Copies:
    def __init__(self, send_sem, recv_sem):
        self.send_sem, self.recv_sem = send_sem, recv_sem
        self.made, self.arrived = {}, set()

    def send(self, name, src, dst, device):
        i = len(self.made)
        copy = pltpu.make_async_remote_copy(
            src_ref=src, dst_ref=dst, send_sem=self.send_sem.at[i], recv_sem=self.recv_sem.at[i],
            device_id=device, device_id_type=MESH,
        )
        copy.start()
        self.made[name] = copy

    def wait(self, *names):
        for name in names:
            if name not in self.arrived:
                self.arrived.add(name)
                self.made[name].wait_recv()

    def finish(self):
        for name, copy in self.made.items():
            self.wait(name)
            copy.wait_send()


def kernel(
    patches_hbm, embed_hbm, conv_hbm, up_hbm, down_hbm, embed_bias_hbm, conv_bias_hbm, gain_hbm, up_bias_hbm, down_bias_hbm,
    out_ref,
    wc, wu, wd, bu, patches, we, vecs, ub, act, embedded, views, left, right, first, last, total, normed,
    local_sem, send_sem, recv_sem,
):
    lon, lat = lax.axis_index("lon"), lax.axis_index("lat")
    z, y_lo, core = lon // 4, (lon // 2) % 2, lon % 2
    y_hi, x = lat // NX, lat % NX

    def device(x, y_hi, z, y_lo, core):
        return {"lon": z * 4 + y_lo * 2 + core, "lat": y_hi * NX + x}

    def along_x(d):
        return (x + d + NX) % NX

    def along_z(d):
        return (z + d + NZ) % NZ

    right_x, left_x = device(along_x(1), y_hi, z, y_lo, core), device(along_x(-1), y_hi, z, y_lo, core)
    up_z, down_z = device(x, y_hi, along_z(1), y_lo, core), device(x, y_hi, along_z(-1), y_lo, core)
    across_hi = device(x, 1 - y_hi, z, 1 - y_lo, core)
    across_lo = device(x, y_hi, z, 1 - y_lo, core)
    twin = device(x, y_hi, z, y_lo, 1 - core)

    def token(dlat, dlon):
        return {"lon": (lon + dlon + 32) % 32, "lat": (lat + dlat + 8) % 8}

    around = [token(a, b) for a in (-1, 0, 1) for b in (-1, 0, 1) if a or b]

    local = {}

    def fetch(name, src, dst):
        local[name] = pltpu.make_async_copy(src, dst, local_sem.at[len(local)])
        local[name].start()

    fetch("patches", patches_hbm, patches)
    fetch("embed", embed_hbm, we)
    for i, vec in enumerate((embed_bias_hbm, conv_bias_hbm, gain_hbm, down_bias_hbm)):
        fetch(("vec", i), vec, vecs.at[i])
    fetch("up_bias", up_bias_hbm, ub)
    fetch("conv", conv_hbm.at[:, core], wc.at[:, y_hi, x, core])
    fetch("up", up_hbm, wu.at[z, y_lo, core])
    fetch("down", down_hbm, wd.at[z, y_lo, core])

    barrier = pltpu.get_barrier_semaphore()
    partners = [right_x, left_x, up_z, down_z, across_hi, across_lo, twin] + around
    for partner in partners:
        pl.semaphore_signal(barrier, inc=1, device_id=partner, device_id_type=MESH)
    pl.semaphore_wait(barrier, len(partners))

    net = Copies(send_sem, recv_sem)
    taps = wc.reshape(TAPS, WIDTH, WIDTH)
    links = {1: right_x, -1: left_x}
    z_links = {"p": (1, up_z), "m": (-1, down_z)}

    def own(t):
        src, dst = conv_hbm.at[t, core], wc.at[t, y_hi, x, core]
        net.send(("own_hi", t), src, dst, across_hi)
        net.send(("own_x", t, 1), src, dst, right_x)
        net.send(("own_x", t, -1), src, dst, left_x)

    def across(t):
        net.wait(("own_hi", t))
        block = wc.at[t, 1 - y_hi, x, core]
        for d, link in links.items():
            net.send(("other_x", t, d), block, block, link)

    def near(t):
        for d in links:
            net.wait(("own_x", t, d))
            if Y_FIRST[t]:
                net.wait(("other_x", t, d))
        d = WAY[t]
        block = wc.at[t, :, along_x(-d), core] if Y_FIRST[t] else wc.at[t, y_hi, along_x(-d), core]
        net.send(("far", t), block, block, links[d])
        if not Y_FIRST[t]:
            for d in links:
                block = wc.at[t, y_hi, along_x(-d), core]
                net.send(("near_hi", t, d), block, block, across_hi)

    def far(t):
        net.wait(("far", t))
        if not Y_FIRST[t]:
            block = wc.at[t, y_hi, along_x(2), core]
            net.send(("far_hi", t), block, block, across_hi)

    def share(t):
        net.wait(("far", t))
        if not Y_FIRST[t]:
            net.wait(("own_hi", t), ("near_hi", t, 1), ("near_hi", t, -1), ("far_hi", t))
        if "conv" in local:
            local.pop("conv").wait()
        block = wc.at[t, :, :, core]
        net.send(("share", t), block, block, twin)

    def conv(t):
        net.wait(("share", t))
        if "halo" not in local:
            local["halo"] = None
            frame()
        a, b = t // 3, t % 3

        @pl.loop(0, WIDTH // TILE)
        def _(i):
            columns = pl.ds(pl.multiple_of(i * TILE, TILE), TILE)
            weight = taps[t, columns]
            term = nt(views[b, a * COLS : a * COLS + TOKENS], weight)
            if t == 0:
                total[:, columns] = term
            else:
                total[:, columns] += term

    def mlp():
        net.send("up_lo", up_hbm, wu.at[z, y_lo, core], across_lo)
        for s, (_, link) in z_links.items():
            net.send(("up_own", s), up_hbm, wu.at[z, y_lo, core], link)
        for s, (_, link) in z_links.items():
            net.send(("down", 1, s), down_hbm, wd.at[z, y_lo, core], link)
        net.send(("down_lo", 0), down_hbm, wd.at[z, y_lo, core], across_lo)
        local.pop("up_bias").wait()
        bu[z, y_lo, core] = pltpu.roll(ub[...], UNITS * (2 * y_lo + core), 1)
        piece = bu.at[z, y_lo, core]
        net.send("bias_lo", piece, piece, across_lo)
        for s, (_, link) in z_links.items():
            net.send(("bias_own", s), piece, piece, link)

    def mlp_y():
        net.wait("up_lo", "bias_lo")
        block, piece = wu.at[z, 1 - y_lo, core], bu.at[z, 1 - y_lo, core]
        for s, (_, link) in z_links.items():
            net.send(("up_other", s), block, block, link)
            net.send(("bias_other", s), piece, piece, link)

    def wait_up(k, s):
        if k == 1:
            net.wait(("up_own", s), ("up_other", s), ("bias_own", s), ("bias_other", s))
        else:
            net.wait(("up", k, s))
            if k < 4 or s == "p":
                net.wait(("bias", k, s))

    def up(k, s):
        wait_up(k, s)
        if k < 4:
            d, link = z_links[s]
            block, piece = wu.at[along_z(-d * k), :, core], bu.at[along_z(-d * k), :, core]
            if k == 3:
                block = block.at[:, pl.ds(0 if s == "p" else HALF, HALF)]
            net.send(("up", k + 1, s), block, block, link)
            if k < 3 or s == "p":
                net.send(("bias", k + 1, s), piece, piece, link)

    def down(k, s):
        net.wait(("down", k, s))
        if k < 4:
            d, link = z_links[s]
            block = wd.at[along_z(-d * k), y_lo, core]
            part = block if k < 3 else block.at[pl.ds(0 if s == "p" else HALF, HALF)]
            net.send(("down", k + 1, s), part, part, link)
            net.send(("down_lo", k, s), block, block, across_lo)

    def down_far():
        net.wait(("down", 4, "p"), ("down", 4, "m"))
        block = wd.at[along_z(4), y_lo, core]
        net.send(("down_lo", 4), block, block, across_lo)

    def share_up(k, s="p"):
        if k == 0:
            net.wait("up_lo", "bias_lo")
            local.pop("up").wait()
        else:
            wait_up(k, s)
        if k == 4:
            wait_up(k, "m")
        d = z_links[s][0]
        block, piece = wu.at[along_z(-d * k), :, core], bu.at[along_z(-d * k), :, core]
        net.send(("share_up", k, s), block, block, twin)
        net.send(("share_bias", k, s), piece, piece, twin)

    def share_down(k, s="p"):
        if k == 0:
            net.wait(("down_lo", 0))
            local.pop("down").wait()
        elif k == 4:
            net.wait(("down_lo", 4), ("down", 4, "p"), ("down", 4, "m"))
        else:
            net.wait(("down_lo", k, s), ("down", k, s))
        block = wd.at[along_z(-z_links[s][0] * k), :, core]
        net.send(("share_down", k, s), block, block, twin)

    def embed():
        for name in ("patches", "embed", *(("vec", i) for i in range(4))):
            local.pop(name).wait()

        @pl.loop(0, WIDTH // TILE)
        def _(i):
            columns = pl.ds(pl.multiple_of(i * TILE, TILE), TILE)
            value = jnp.dot(patches[...], we[:, columns], preferred_element_type=jnp.float32)
            value = (value + vecs[0, :, columns]).astype(jnp.bfloat16)
            embedded[:, columns] = value
            value = gelu(value.astype(jnp.float32)).astype(jnp.bfloat16)
            views[1, COLS : COLS + TOKENS, columns] = value
            act[:, columns] = value.astype(jnp.float32)

        for i in range(ROWS):
            first[i : i + 1] = act[i * COLS : i * COLS + 1]
            last[i : i + 1] = act[i * COLS + COLS - 1 : i * COLS + COLS]
        net.send("row_after", views.at[1, pl.ds(TOKENS, COLS)], views.at[1, pl.ds(0, COLS)], token(1, 0))
        net.send("row_before", views.at[1, pl.ds(COLS, COLS)], views.at[1, pl.ds(TOKENS + COLS, COLS)], token(-1, 0))
        for a in (0, 1, -1):
            net.send(("col_after", a), last, left.at[1 - a], token(a, 1))
            net.send(("col_before", a), first, right.at[1 - a], token(a, -1))

    def frame():
        net.wait("row_after", "row_before", *((n, a) for n in ("col_after", "col_before") for a in (0, 1, -1)))
        place = lax.broadcasted_iota(jnp.int32, (COLS, WIDTH), 0)
        for i in range(ROWS + 2):
            rows = slice(i * COLS, (i + 1) * COLS)
            slot, row = (0, ROWS - 1) if i == 0 else (2, 0) if i == ROWS + 1 else (1, i - 1)
            if 0 < i <= ROWS:
                middle = act[(i - 1) * COLS : i * COLS]
            else:
                middle = views[1, rows].astype(jnp.float32)
            before = jnp.where(place == 0, left[slot, row : row + 1], pltpu.roll(middle, 1, 0))
            after = jnp.where(place == COLS - 1, right[slot, row : row + 1], pltpu.roll(middle, COLS - 1, 0))
            if i in (0, ROWS + 1):
                inside = lat > 0 if i == 0 else lat < 7
                middle, before, after = (jnp.where(inside, v, 0.0) for v in (middle, before, after))
                views[1, rows] = middle.astype(jnp.bfloat16)
            views[0, rows] = before.astype(jnp.bfloat16)
            views[2, rows] = after.astype(jnp.bfloat16)

    steps = dict(
        own=own, across=across, near=near, far=far, share=share, conv=conv, mlp=mlp, mlp_y=mlp_y, up=up, down=down,
        down_far=down_far, share_up=share_up, share_down=share_down, embed=embed,
    )
    for name, *args in ORDER:
        steps[name](*args)

    for k, s in ((0, "p"), (1, "p"), (1, "m"), (2, "p"), (2, "m"), (3, "p"), (3, "m"), (4, "p")):
        net.wait(("share_up", k, s), ("share_bias", k, s), ("share_down", k, s))

    mixed = (embedded[...].astype(jnp.float32) + total[...] + vecs[1]).astype(jnp.bfloat16).astype(jnp.float32)
    center = jnp.mean(mixed, axis=1, keepdims=True)
    spread = jnp.mean((mixed - center) ** 2, axis=1, keepdims=True)
    normed[...] = ((mixed - center) * lax.rsqrt(spread + 1e-05) * vecs[2]).astype(jnp.bfloat16)
    total[...] = mixed + vecs[3]

    @pl.loop(0, NZ)
    def _(j):
        bias = jnp.sum(bu[j].reshape(4, 8, 4 * UNITS), axis=0)[:1]
        hidden = gelu(nt(normed[...], wu[j].reshape(4 * UNITS, WIDTH)) + bias).astype(jnp.bfloat16)
        total[...] += jnp.dot(hidden, wd[j].reshape(4 * UNITS, WIDTH), preferred_element_type=jnp.float32)

    out_ref[...] = total[...].astype(jnp.bfloat16)
    net.finish()


def body(patches, embed_weight, embed_bias, conv_weight, conv_bias, norm_gain, up_weight, up_bias, down_weight, down_bias):
    rows, cols, inputs = patches.shape
    bf16, f32 = jnp.bfloat16, jnp.float32
    out = pl.pallas_call(
        kernel,
        out_shape=jax.ShapeDtypeStruct((TOKENS, WIDTH), bf16),
        in_specs=[pl.BlockSpec(memory_space=pl.ANY)] * 10,
        out_specs=pl.BlockSpec(memory_space=pltpu.VMEM),
        scratch_shapes=[
            pltpu.VMEM((TAPS, 2, NX, 2, HALF, WIDTH), bf16),
            pltpu.VMEM((NZ, 2, 2, UNITS, WIDTH), bf16),
            pltpu.VMEM((NZ, 2, 2, UNITS, WIDTH), bf16),
            pltpu.VMEM((NZ, 2, 2, 8, 4 * UNITS), f32),
            pltpu.VMEM((TOKENS, inputs), bf16),
            pltpu.VMEM((inputs, WIDTH), bf16),
            pltpu.VMEM((4, 1, WIDTH), f32),
            pltpu.VMEM((8, 4 * UNITS), f32),
            pltpu.VMEM((TOKENS, WIDTH), f32),
            pltpu.VMEM((TOKENS, WIDTH), bf16),
            pltpu.VMEM((3, TOKENS + 2 * COLS, WIDTH), bf16),
            pltpu.VMEM((3, ROWS, WIDTH), f32),
            pltpu.VMEM((3, ROWS, WIDTH), f32),
            pltpu.VMEM((ROWS, WIDTH), f32),
            pltpu.VMEM((ROWS, WIDTH), f32),
            pltpu.VMEM((TOKENS, WIDTH), f32),
            pltpu.VMEM((TOKENS, WIDTH), bf16),
            pltpu.SemaphoreType.DMA((10,)),
            pltpu.SemaphoreType.DMA((160,)),
            pltpu.SemaphoreType.DMA((160,)),
        ],
        compiler_params=pltpu.CompilerParams(collective_id=0, has_side_effects=True, vmem_limit_bytes=56 << 20),
        cost_estimate=pl.CostEstimate(flops=5_570_000_000, bytes_accessed=5_000_000, transcendentals=1_000_000),
        name="block",
    )(
        patches.reshape(TOKENS, inputs),
        embed_weight,
        jnp.swapaxes(conv_weight, 2, 3).reshape(TAPS, 2, HALF, WIDTH),
        up_weight.T,
        down_weight.T,
        embed_bias.reshape(1, WIDTH),
        conv_bias.reshape(1, WIDTH),
        norm_gain.reshape(1, WIDTH),
        jnp.pad(up_bias, ((0, 7), (0, 3 * UNITS))),
        down_bias.reshape(1, WIDTH),
    )
    return out.reshape(rows, cols, WIDTH)


def solution(mesh):
    in_specs = (
        P("lat", "lon", None),
        P(),
        P(),
        P(None, None, None, "lat"),
        P(),
        P(),
        P(None, "lon"),
        P(None, "lon"),
        P(None, "lon"),
        P(),
    )
    return jax.shard_map(body, mesh=mesh, in_specs=in_specs, out_specs=P("lat", "lon", None), check_vma=False)
```

time: 305 us -> 73.9 us (0.24)
  waiting for transfers between devices: 148 us -> 0 us
  blocking collectives: 107 us -> 0 us
  Pallas kernels: 0 us -> 65.5 us
  matrix products: 20.4 us -> 0 us
  between operations: 14 us -> 0.01 us
  starting transfers between devices: 7.86 us -> 0 us
  local copies, waits for them, and re-layouts: 2.97 us -> 8.13 us
  other arithmetic: 4.01 us -> 0 us
    all_gather x3 -> x0, waiting for transfers between devices: 142 us -> none  [the longest x1 69.4 us: body(): down_all = lax.all_gather(down_weight.T, 'lon', axis=0, tiled=True)]
    unnamed x1 -> x0, blocking collectives: 107 us -> none
    pallas_call x0 -> x1, Pallas kernels: none -> 65.5 us  [body(): pl.pallas_call(kernel, out_shape=jax.ShapeDtypeStruct((TOKENS, WIDTH), bf...]
    dot_general x11 -> x0, matrix products: 20.4 us -> none  [the longest x9 11.1 us: stencil(): jnp.dot(window, kernel[row_off, col_off], preferred_element_type=jnp.floa...]
    ppermute x4 -> x0, starting transfers between devices: 7.79 us -> none  [the longest x2 5.85 us: extended(): before = lax.ppermute(last, axis, up)]
    reshape x0 -> x4, local copies, waits for them, and re-layouts: none -> 5.11 us  [the longest x1 1.28 us: body(): down_bias.reshape(1, WIDTH)]
    ppermute x4 -> x0, waiting for transfers between devices: 3.79 us -> none  [the longest x2 3.78 us: extended(): after = lax.ppermute(leading, axis, down)]
  transfers between devices with their start and end apart: 7 -> 0, of which waited for: 4 -> 0; matrix products, arithmetic and copies ran while one was open for 6% -> 0% of each run, Pallas kernels for 0% -> 0%
where the time goes in v2:
time: 73.9 us; the launch traced here: 73.6 us
  Pallas kernels  65.5 us (89%)
  local copies, waits for them, and re-layouts  8.13 us (11%)
    pallas_call x1, Pallas kernels, body(): pl.pallas_call(kernel, out_shape=jax.ShapeDtypeStruct((TOKENS, WIDTH), bf...  65.5 us
    unnamed x1, local copies, waits for them, and re-layouts  1.77 us

profile of v2, /device:TPU:1, one launch (start us, length us, event | category | flops | bytes accessed | tf_op | source)
XLA Modules:
  0.0 73.6 jit_solution(12318587538835818834)
XLA Ops:
  0.0 1.3 %reshape.23.embed_bias_hbm = f32[1,768]{1,0:T(1,128)} reshape(f32[768]{0:T(1024)} %param.12) | data formatting | bytes 6144 | tf_op jit(solution)/shard_map/reshape | solution.py:363
  1.3 1.3 %reshape.24.conv_bias_hbm = f32[1,768]{1,0:T(1,128)} reshape(f32[768]{0:T(1024)} %param.14) | data formatting | bytes 6144 | tf_op jit(solution)/shard_map/reshape | solution.py:364
  2.5 1.3 %reshape.25.gain_hbm = f32[1,768]{1,0:T(1,128)} reshape(f32[768]{0:T(1024)} %param.15) | data formatting | bytes 6144 | tf_op jit(solution)/shard_map/reshape | solution.py:365
  3.8 1.3 %reshape.26.down_bias_hbm = f32[1,768]{1,0:T(1,128)} reshape(f32[768]{0:T(1024)} %param.19) | data formatting | bytes 6144 | tf_op jit(solution)/shard_map/reshape | solution.py:367
  5.1 1.3 %pad.4.up_bias_hbm = f32[8,384]{1,0:T(8,128)} pad(f32[1,96]{1,0:T(1,128)} %param.17, f32[]{:T(128)} %constant.2.clone.1), padding=0_7x0_288 | pad | bytes 12676 | tf_op jit(solution)/shard_map/jit(_pad)/pad | solution.py:366
  6.4 65.5 %block.1 = bf16[256,768]{1,0:T(8,128)(2,1)} custom-call(bf16[256,1104]{1,0:T(8,128)(2,1)} %bitcast.9, bf16[1104,768]{1,0:T(8,128)(2,1)} %embed_hbm.1, bf16[9,2,48,768]{3,2,1,0:T(8,128)(2,1)} %bitcast.8, bf16[96,768]{1,0:T(8,128)(2,1)} %bitcast.10, bf16[96,768]{1,0:T(8,128)(2,1)} %bitcast.11, f32[1,768]{1,0:T(1,128)} %reshape.23.embed_bias_hbm, ...), custom_call_target="tpu_custom_call" | custom-call | flops 5569999872 | bytes 5000000 | tf_op jit(solution)/shard_map/block/pallas_call | solution.py:327
  71.9 1.8 %copy.12 = bf16[8,32,768]{2,1,0:T(8,128)(2,1)} copy(bf16[8,32,768]{2,1,0:T(8,128)(2,1)} %bitcast.7) | data formatting | bytes 786432

commit v3 on v2

--- a/solution.py
+++ b/solution.py
@@ -65,9 +65,10 @@
 def kernel(
     patches_hbm, embed_hbm, conv_hbm, up_hbm, down_hbm, embed_bias_hbm, conv_bias_hbm, gain_hbm, up_bias_hbm, down_bias_hbm,
     out_ref,
-    wc, wu, wd, bu, patches, we, vecs, ub, act, embedded, views, left, right, first, last, total, normed,
+    wc, wu, wd, bu, patches, we, v0, v1, v2, v3, ub, act, embedded, views, left, right, first, last, total, normed, hidden, bias,
     local_sem, send_sem, recv_sem,
 ):
+    vecs = (v0, v1, v2, v3)
     lon, lat = lax.axis_index("lon"), lax.axis_index("lat")
     z, y_lo, core = lon // 4, (lon // 2) % 2, lon % 2
     y_hi, x = lat // NX, lat % NX
@@ -101,7 +102,7 @@
     fetch("patches", patches_hbm, patches)
     fetch("embed", embed_hbm, we)
     for i, vec in enumerate((embed_bias_hbm, conv_bias_hbm, gain_hbm, down_bias_hbm)):
-        fetch(("vec", i), vec, vecs.at[i])
+        fetch(("vec", i), vec, vecs[i])
     fetch("up_bias", up_bias_hbm, ub)
     fetch("conv", conv_hbm.at[:, core], wc.at[:, y_hi, x, core])
     fetch("up", up_hbm, wu.at[z, y_lo, core])
@@ -165,15 +166,8 @@
             frame()
         a, b = t // 3, t % 3
 
-        @pl.loop(0, WIDTH // TILE)
-        def _(i):
-            columns = pl.ds(pl.multiple_of(i * TILE, TILE), TILE)
-            weight = taps[t, columns]
-            term = nt(views[b, a * COLS : a * COLS + TOKENS], weight)
-            if t == 0:
-                total[:, columns] = term
-            else:
-                total[:, columns] += term
+        term = nt(views[b, a * COLS : a * COLS + TOKENS], taps[t])
+        total[...] = term if t == 0 else total[...] + term
 
     def mlp():
         net.send("up_lo", up_hbm, wu.at[z, y_lo, core], across_lo)
@@ -183,7 +177,9 @@
             net.send(("down", 1, s), down_hbm, wd.at[z, y_lo, core], link)
         net.send(("down_lo", 0), down_hbm, wd.at[z, y_lo, core], across_lo)
         local.pop("up_bias").wait()
-        bu[z, y_lo, core] = pltpu.roll(ub[...], UNITS * (2 * y_lo + core), 1)
+        spread = jnp.concatenate([ub[...], jnp.zeros((1, 3 * UNITS), jnp.float32)], axis=1)
+        spread = jnp.broadcast_to(spread, (8, 4 * UNITS))
+        bu[z, y_lo, core] = pltpu.roll(spread, UNITS * (2 * y_lo + core), 1)
         piece = bu.at[z, y_lo, core]
         net.send("bias_lo", piece, piece, across_lo)
         for s, (_, link) in z_links.items():
@@ -257,16 +253,12 @@
         for name in ("patches", "embed", *(("vec", i) for i in range(4))):
             local.pop(name).wait()
 
-        @pl.loop(0, WIDTH // TILE)
-        def _(i):
-            columns = pl.ds(pl.multiple_of(i * TILE, TILE), TILE)
-            value = jnp.dot(patches[...], we[:, columns], preferred_element_type=jnp.float32)
-            value = (value + vecs[0, :, columns]).astype(jnp.bfloat16)
-            embedded[:, columns] = value
-            value = gelu(value.astype(jnp.float32)).astype(jnp.bfloat16)
-            views[1, COLS : COLS + TOKENS, columns] = value
-            act[:, columns] = value.astype(jnp.float32)
-
+        value = jnp.dot(patches[...], we[...], preferred_element_type=jnp.float32)
+        value = (value + vecs[0][...]).astype(jnp.bfloat16)
+        embedded[...] = value
+        value = gelu(value.astype(jnp.float32)).astype(jnp.bfloat16)
+        views[1, COLS : COLS + TOKENS] = value
+        act[...] = value.astype(jnp.float32)
         for i in range(ROWS):
             first[i : i + 1] = act[i * COLS : i * COLS + 1]
             last[i : i + 1] = act[i * COLS + COLS - 1 : i * COLS + COLS]
@@ -305,17 +297,20 @@
     for k, s in ((0, "p"), (1, "p"), (1, "m"), (2, "p"), (2, "m"), (3, "p"), (3, "m"), (4, "p")):
         net.wait(("share_up", k, s), ("share_bias", k, s), ("share_down", k, s))
 
-    mixed = (embedded[...].astype(jnp.float32) + total[...] + vecs[1]).astype(jnp.bfloat16).astype(jnp.float32)
+    mixed = (embedded[...].astype(jnp.float32) + total[...] + vecs[1][...]).astype(jnp.bfloat16).astype(jnp.float32)
     center = jnp.mean(mixed, axis=1, keepdims=True)
     spread = jnp.mean((mixed - center) ** 2, axis=1, keepdims=True)
-    normed[...] = ((mixed - center) * lax.rsqrt(spread + 1e-05) * vecs[2]).astype(jnp.bfloat16)
-    total[...] = mixed + vecs[3]
-
-    @pl.loop(0, NZ)
-    def _(j):
-        bias = jnp.sum(bu[j].reshape(4, 8, 4 * UNITS), axis=0)[:1]
-        hidden = gelu(nt(normed[...], wu[j].reshape(4 * UNITS, WIDTH)) + bias).astype(jnp.bfloat16)
-        total[...] += jnp.dot(hidden, wd[j].reshape(4 * UNITS, WIDTH), preferred_element_type=jnp.float32)
+    normed[...] = ((mixed - center) * lax.rsqrt(spread + 1e-05) * vecs[2][...]).astype(jnp.bfloat16)
+    total[...] = mixed + vecs[3][...]
+
+    for j in range(NZ):
+        units = slice(j * 4 * UNITS, (j + 1) * 4 * UNITS)
+        bias[:, units] = jnp.sum(bu[j].reshape(4, 8, 4 * UNITS), axis=0)
+    ups, downs = wu.reshape(NZ * 4 * UNITS, WIDTH), wd.reshape(NZ * 4 * UNITS, WIDTH)
+    for j in range(NZ * 4 * UNITS // TILE):
+        units = slice(j * TILE, (j + 1) * TILE)
+        hidden[:, units] = gelu(nt(normed[...], ups[units]) + bias[:1, units]).astype(jnp.bfloat16)
+    total[...] += jnp.dot(hidden[...], downs[...], preferred_element_type=jnp.float32)
 
     out_ref[...] = total[...].astype(jnp.bfloat16)
     net.finish()
@@ -336,8 +331,8 @@
             pltpu.VMEM((NZ, 2, 2, 8, 4 * UNITS), f32),
             pltpu.VMEM((TOKENS, inputs), bf16),
             pltpu.VMEM((inputs, WIDTH), bf16),
-            pltpu.VMEM((4, 1, WIDTH), f32),
-            pltpu.VMEM((8, 4 * UNITS), f32),
+            *[pltpu.VMEM((WIDTH,), f32)] * 4,
+            pltpu.VMEM((1, UNITS), f32),
             pltpu.VMEM((TOKENS, WIDTH), f32),
             pltpu.VMEM((TOKENS, WIDTH), bf16),
             pltpu.VMEM((3, TOKENS + 2 * COLS, WIDTH), bf16),
@@ -347,6 +342,8 @@
             pltpu.VMEM((ROWS, WIDTH), f32),
             pltpu.VMEM((TOKENS, WIDTH), f32),
             pltpu.VMEM((TOKENS, WIDTH), bf16),
+            pltpu.VMEM((TOKENS, NZ * 4 * UNITS), bf16),
+            pltpu.VMEM((8, NZ * 4 * UNITS), f32),
             pltpu.SemaphoreType.DMA((10,)),
             pltpu.SemaphoreType.DMA((160,)),
             pltpu.SemaphoreType.DMA((160,)),
@@ -360,11 +357,11 @@
         jnp.swapaxes(conv_weight, 2, 3).reshape(TAPS, 2, HALF, WIDTH),
         up_weight.T,
         down_weight.T,
-        embed_bias.reshape(1, WIDTH),
-        conv_bias.reshape(1, WIDTH),
-        norm_gain.reshape(1, WIDTH),
-        jnp.pad(up_bias, ((0, 7), (0, 3 * UNITS))),
-        down_bias.reshape(1, WIDTH),
+        embed_bias,
+        conv_bias,
+        norm_gain,
+        up_bias,
+        down_bias,
     )
     return out.reshape(rows, cols, WIDTH)
 

time: 73.9 us -> 63.8 us (0.86)
  local copies, waits for them, and re-layouts: 8.13 us -> 1.77 us
  Pallas kernels: 65.5 us -> 61.9 us
    reshape x4 -> x0, local copies, waits for them, and re-layouts: 5.11 us -> none  [the longest x1 1.28 us: body(): down_bias.reshape(1, WIDTH)]
    pallas_call x1, Pallas kernels: 65.5 us -> 61.9 us  [body(): pl.pallas_call(kernel, out_shape=jax.ShapeDtypeStruct((TOKENS, WIDTH), bf...]
    pad x1 -> x0, local copies, waits for them, and re-layouts: 1.26 us -> none  [body(): jnp.pad(up_bias, ((0, 7), (0, 3 * UNITS)))]
where the time goes in v3:
time: 63.8 us; the launch traced here: 63.7 us
  Pallas kernels  61.9 us (97%)
  local copies, waits for them, and re-layouts  1.77 us (3%)
    pallas_call x1, Pallas kernels, body(): pl.pallas_call(kernel, out_shape=jax.ShapeDtypeStruct((TOKENS, WIDTH), bf...  61.9 us
    unnamed x1, local copies, waits for them, and re-layouts  1.77 us

profile of v3, /device:TPU:1, one launch (start us, length us, event | category | flops | bytes accessed | tf_op | source)
XLA Modules:
  0.0 63.7 jit_solution(857040949092417452)
XLA Ops:
  0.0 61.9 %block.1 = bf16[256,768]{1,0:T(8,128)(2,1)} custom-call(bf16[256,1104]{1,0:T(8,128)(2,1)} %bitcast.9, bf16[1104,768]{1,0:T(8,128)(2,1)} %embed_hbm.1, bf16[9,2,48,768]{3,2,1,0:T(8,128)(2,1)} %bitcast.8, bf16[96,768]{1,0:T(8,128)(2,1)} %bitcast.10, bf16[96,768]{1,0:T(8,128)(2,1)} %bitcast.11, f32[768]{0:T(1024)} %embed_bias_hbm.1, f32[768]{0:T(1024)} %conv_bias_hbm.1, ...), custom_call_target="tpu_custom_call" | custom-call | flops 5569999872 | bytes 5000000 | tf_op jit(solution)/shard_map/block/pallas_call | solution.py:322
  61.9 1.8 %copy.12 = bf16[8,32,768]{2,1,0:T(8,128)(2,1)} copy(bf16[8,32,768]{2,1,0:T(8,128)(2,1)} %bitcast.7) | data formatting | bytes 786432

commit v4 on v3

v4 whole, which is shorter than its diff:
```python
import jax
import jax.numpy as jnp
from jax import lax
from jax.experimental import pallas as pl
from jax.experimental.pallas import tpu as pltpu
from jax.sharding import PartitionSpec as P

MESH = pl.DeviceIdType.MESH
NX, NZ = 4, 8
ROWS, COLS, WIDTH, UNITS = 8, 32, 768, 96
TOKENS, HALF, TILE = ROWS * COLS, UNITS // 2, 256
OUT = WIDTH // 2
TAPS = 9
COPIES = 160
WAY = (1, -1, 1, -1, 1, -1, 1, -1, 1)
Y_LINK = {"yd0": "L", "yd4": "L", "yd4m": "L", "ydm": "L", "ydp": "H", "yu0": "L", "yu4": "L", "yum": "H", "yup": "L"}
ORDER = (
    ("mlp",), ("own", 5), ("own", 0), ("embed",), ("own", 1), ("own", 2), ("own", 3), ("own", 4), ("own", 6),
    ("mlp_y",), ("near", 5), ("own", 7), ("up", 1, "p"), ("up", 1, "m"), ("share_up", 0, "p"), ("near", 0),
    ("own", 8), ("halo",), ("near", 1), ("down", 1, "p"), ("down", 1, "m"), ("share_down", 0, "p"), ("near", 2),
    ("other", 1, "p"), ("near", 3), ("other", 1, "m"), ("share_up", 1, "p"), ("near", 4), ("share_down", 1, "m"),
    ("up", 2, "p"), ("up", 2, "m"), ("share_up", 1, "m"), ("near", 6), ("share", 5), ("down", 2, "p"),
    ("down", 2, "m"), ("near", 7), ("frame_other",), ("share", 0), ("conv", 5), ("other", 2, "p"), ("other", 2, "m"),
    ("share_up", 2, "p"), ("near", 8), ("conv", 0), ("share", 1), ("share_down", 1, "p"), ("share", 2), ("conv", 1),
    ("share", 3), ("up", 3, "m"), ("up", 3, "p"), ("share_up", 2, "m"), ("share", 4), ("share_down", 2, "m"),
    ("conv", 2), ("share", 7), ("conv", 3), ("share", 6), ("conv", 4), ("down", 3, "p"), ("down", 3, "m"),
    ("share_down", 2, "p"), ("share", 8), ("conv", 6), ("conv", 7), ("other", 3, "p"), ("other", 3, "m"),
    ("share_up", 3, "p"), ("conv", 8), ("swap",), ("share_up", 3, "m"), ("up", 4, "m"), ("share_down", 3, "p"),
    ("share_down", 3, "m"), ("down", 4, "p"), ("down", 4, "m"), ("share_up", 4, "p"), ("share_down", 4, "p"),
)


def slot(k, s):
    return 7 if k == 4 else 0 if k == 0 else 2 * k - (s == "p")


def gelu(v):
    return 0.5 * v * (1.0 + jnp.tanh(0.7978845608028654 * (v + 0.044715 * (v * v * v))))


def nt(a, b):
    return lax.dot_general(a, b, (((1,), (1,)), ((), ())), preferred_element_type=jnp.float32)


class Copies:
    def __init__(self, send_sem, recv_sem):
        self.send_sem, self.recv_sem = send_sem, recv_sem
        self.made, self.arrived = {}, set()

    def send(self, name, src, dst, device):
        i = len(self.made)
        copy = pltpu.make_async_remote_copy(
            src_ref=src, dst_ref=dst, send_sem=self.send_sem.at[i], recv_sem=self.recv_sem.at[i],
            device_id=device, device_id_type=MESH,
        )
        copy.start()
        self.made[name] = copy

    def wait(self, *names):
        for name in names:
            if name not in self.arrived:
                self.arrived.add(name)
                self.made[name].wait_recv()

    def finish(self):
        for name, copy in self.made.items():
            self.wait(name)
            copy.wait_send()


def kernel(
    patches_hbm, embed_hbm, conv_hbm, up_hbm, down_hbm, embed_bias_hbm, conv_bias_hbm, gain_hbm, up_bias_hbm, down_bias_hbm,
    out_ref,
    wc, wu, wd, bu, patches, we, v0, v1, v2, v3, ub, act, embedded, views, left, right, first, last, edges, total, give, got,
    summed, normed, hidden, bias, local_sem, send_sem, recv_sem,
):
    vecs = (v0, v1, v2, v3)
    lon, lat = lax.axis_index("lon"), lax.axis_index("lat")
    z, y_lo, core = lon // 4, (lon // 2) % 2, lon % 2
    y_hi, x = lat // NX, lat % NX

    def device(x, y_hi, z, y_lo, core):
        return {"lon": z * 4 + y_lo * 2 + core, "lat": y_hi * NX + x}

    def along_x(d):
        return (x + d + NX) % NX

    def along_z(d):
        return (z + d + NZ) % NZ

    x_links = {1: device(along_x(1), y_hi, z, y_lo, core), -1: device(along_x(-1), y_hi, z, y_lo, core)}
    z_links = {"p": device(x, y_hi, along_z(1), y_lo, core), "m": device(x, y_hi, along_z(-1), y_lo, core)}
    pair = device(x, 1 - y_hi, z, 1 - y_lo, core)
    across = device(x, y_hi, z, 1 - y_lo, core)
    y_links = {"L": across, "H": pair}
    twin = device(x, y_hi, z, y_lo, 1 - core)

    def token(dlat, dlon):
        return {"lon": (lon + dlon + 32) % 32, "lat": (lat + dlat + 8) % 8}

    around = [token(a, b) for a in (-1, 0, 1) for b in (-1, 0, 1) if a or b]

    local = {}

    def fetch(name, src, dst):
        local[name] = pltpu.make_async_copy(src, dst, local_sem.at[len(local)])
        local[name].start()

    fetch("patches", patches_hbm, patches)
    fetch("embed", embed_hbm, we)
    for i, vec in enumerate((embed_bias_hbm, conv_bias_hbm, gain_hbm, down_bias_hbm)):
        fetch(("vec", i), vec, vecs[i])
    fetch("up_bias", up_bias_hbm, ub)
    fetch("conv", conv_hbm.at[:, core], wc.at[:, x, core])
    fetch("up", up_hbm, wu.at[0, y_lo, core])
    fetch("down", down_hbm, wd.at[0, y_lo, core])

    barrier = pltpu.get_barrier_semaphore()
    partners = [*x_links.values(), *z_links.values(), pair, across, twin] + around
    for partner in partners:
        pl.semaphore_signal(barrier, inc=1, device_id=partner, device_id_type=MESH)
    pl.semaphore_wait(barrier, len(partners))

    net = Copies(send_sem, recv_sem)
    taps = wc.reshape(TAPS, OUT, WIDTH)

    def own(t):
        for d, link in x_links.items():
            net.send(("own_x", t, d), conv_hbm.at[t, core], wc.at[t, x, core], link)

    def near(t):
        d = WAY[t]
        net.wait(("own_x", t, d))
        block = wc.at[t, along_x(-d), core]
        net.send(("far", t), block, block, x_links[d])

    def share(t):
        net.wait(("own_x", t, 1), ("own_x", t, -1), ("far", t))
        if "conv" in local:
            local.pop("conv").wait()
        block = wc.at[t, :, core]
        net.send(("share", t), block, block, twin)

    def conv(t):
        net.wait(("share", t))
        a, b = t // 3, t % 3
        rows = slice(a * COLS, a * COLS + TOKENS)
        term = nt(jnp.concatenate([views[0, b, rows], views[1, b, rows]]), taps[t])
        total[...] = term if t == 5 else total[...] + term

    def swap():
        give[...] = total[TOKENS:].astype(jnp.bfloat16)
        net.send("swap", give, got, pair)

    def mlp():
        near_half = pl.ds(0, HALF)
        net.send("up_lo", up_hbm.at[near_half], wu.at[0, y_lo, core, near_half], across)
        for s, link in z_links.items():
            net.send(("u", 1, s), up_hbm, wu.at[slot(1, s), y_lo, core], link)
        for s, link in z_links.items():
            net.send(("d", 1, s), down_hbm, wd.at[slot(1, s), y_lo, core], link)
        far_half = pl.ds(HALF, HALF)
        net.send(("yu", 0, "p"), up_hbm.at[far_half], wu.at[0, y_lo, core, far_half], y_links[Y_LINK["yu0"]])
        net.send(("yd", 0, "p"), down_hbm, wd.at[0, y_lo, core], y_links[Y_LINK["yd0"]])
        local.pop("up_bias").wait()
        row = jnp.concatenate([ub[...], jnp.zeros((1, 3 * UNITS), jnp.float32)], axis=1)
        row = jnp.broadcast_to(row, (8, 4 * UNITS))
        bu[0, y_lo, core] = pltpu.roll(row, UNITS * (2 * y_lo + core), 1)
        piece = bu.at[0, y_lo, core]
        net.send("bias_lo", piece, piece, across)
        for s, link in z_links.items():
            net.send(("bias_own", s), piece, bu.at[slot(1, s), y_lo, core], link)

    def mlp_y():
        net.wait("up_lo", "bias_lo")
        half = pl.ds(0, HALF)
        for s, link in z_links.items():
            net.send(("v", 1, s), wu.at[0, 1 - y_lo, core, half], wu.at[slot(1, s), 1 - y_lo, core, half], link)
            net.send(("bias_other", s), bu.at[0, 1 - y_lo, core], bu.at[slot(1, s), 1 - y_lo, core], link)

    def part(k, s):
        return pl.ds(0, UNITS) if k < 3 else pl.ds(0 if s == "p" else HALF, HALF)

    def up(k, s):
        net.wait(("u", k, s))
        here = wu.at[slot(k, s), y_lo, core]
        if k < 4:
            there = wu.at[slot(k + 1, s), y_lo, core]
            net.send(("u", k + 1, s), here.at[part(k, s)], there.at[part(k, s)], z_links[s])
        block = here.at[pl.ds(HALF, HALF)]
        if k < 4:
            net.send(("yu", k, s), block, block, y_links[Y_LINK["yu" + s]])
        else:
            net.send(("yu", k, "p"), block, block, y_links[Y_LINK["yu4"]])

    def down(k, s):
        net.wait(("d", k, s))
        here = wd.at[slot(k, s), y_lo, core]
        if k < 4:
            there = wd.at[slot(k + 1, s), y_lo, core]
            net.send(("d", k + 1, s), here.at[part(k, s)], there.at[part(k, s)], z_links[s])
            net.send(("yd", k, s), here, here, y_links[Y_LINK["yd" + s]])
        else:
            block = here.at[part(3, s)]
            net.send(("yd", k, s), block, block, y_links[Y_LINK["yd4" if s == "p" else "yd4m"]])

    def wait_other(k, s):
        if k == 1:
            net.wait(("v", 1, s), ("bias_own", s), ("bias_other", s))
        elif k < 4:
            net.wait(("v", k, s), ("bias", k, s))
        else:
            net.wait(("v", 4, "p"), ("bias", 4, "m"))

    def other(k, s):
        wait_other(k, s)
        half = pl.ds(0, HALF)
        if k < 3 or s == "p":
            block, there = wu.at[slot(k, s), 1 - y_lo, core, half], wu.at[slot(k + 1, s), 1 - y_lo, core, half]
            net.send(("v", k + 1, s), block, there, z_links[s])
        if k < 3 or s == "m":
            net.send(("bias", k + 1, s), bu.at[slot(k, s), :, core], bu.at[slot(k + 1, s), :, core], z_links[s])

    def share_up(k, s):
        if k == 0:
            net.wait("up_lo", "bias_lo", ("yu", 0, "p"))
            local.pop("up").wait()
        else:
            wait_other(k, s)
            net.wait(("u", k, s), ("yu", k, s))
        if k == 4:
            net.wait(("u", 4, "m"))
        block, piece = wu.at[slot(k, s), :, core], bu.at[slot(k, s), :, core]
        net.send(("share_up", k, s), block, block, twin)
        net.send(("share_bias", k, s), piece, piece, twin)

    def share_down(k, s):
        net.wait(("yd", k, s))
        if k == 0:
            local.pop("down").wait()
        else:
            net.wait(("d", k, s))
        if k == 4:
            net.wait(("d", 4, "m"), ("yd", 4, "m"))
        block = wd.at[slot(k, s), :, core]
        net.send(("share_down", k, s), block, block, twin)

    middle_rows = pl.ds(COLS, TOKENS)

    def embed():
        for name in ("patches", "embed", *(("vec", i) for i in range(4))):
            local.pop(name).wait()
        value = jnp.dot(patches[...], we[...], preferred_element_type=jnp.float32)
        value = (value + vecs[0][...]).astype(jnp.bfloat16)
        embedded[...] = value
        value = gelu(value.astype(jnp.float32)).astype(jnp.bfloat16)
        views[0, 1, COLS : COLS + TOKENS] = value
        act[...] = value.astype(jnp.float32)
        net.send("act", views.at[0, 1, middle_rows], views.at[1, 1, middle_rows], pair)
        for i in range(ROWS):
            first[i : i + 1] = act[i * COLS : i * COLS + 1]
            last[i : i + 1] = act[i * COLS + COLS - 1 : i * COLS + COLS]
        net.send("row_after", views.at[0, 1, pl.ds(TOKENS, COLS)], views.at[0, 1, pl.ds(0, COLS)], token(1, 0))
        net.send("row_before", views.at[0, 1, pl.ds(COLS, COLS)], views.at[0, 1, pl.ds(TOKENS + COLS, COLS)], token(-1, 0))
        for a in (0, 1, -1):
            net.send(("col_after", a), last, left.at[1 - a], token(a, 1))
            net.send(("col_before", a), first, right.at[1 - a], token(a, -1))

    def halo():
        net.wait("row_after", "row_before", *((n, a) for n in ("col_after", "col_before") for a in (0, 1, -1)))
        north, south = lat > 0, lat < 7
        none = jnp.zeros((6, WIDTH), jnp.float32)
        edges[0, :COLS] = jnp.where(north, views[0, 1, :COLS].astype(jnp.float32), 0.0).astype(jnp.bfloat16)
        edges[0, COLS : 2 * COLS] = jnp.where(south, views[0, 1, TOKENS + COLS :].astype(jnp.float32), 0.0).astype(jnp.bfloat16)
        for i, side in enumerate((left, right)):
            above = jnp.where(north, side[0, ROWS - 1 :], 0.0)
            below = jnp.where(south, side[2, :1], 0.0)
            column = jnp.concatenate([above, side[1], below, none], axis=0)
            edges[0, 2 * COLS + 16 * i : 2 * COLS + 16 * (i + 1)] = column.astype(jnp.bfloat16)
        net.send("edge", edges.at[0], edges.at[1], pair)
        frame(0)

    def frame_other():
        net.wait("act", "edge")
        frame(1)

    def frame(own_or_pair):
        place = lax.broadcasted_iota(jnp.int32, (COLS, WIDTH), 0)
        view, edge = views.at[own_or_pair], edges.at[own_or_pair]
        view[1, :COLS] = edge[:COLS]
        view[1, TOKENS + COLS :] = edge[COLS : 2 * COLS]
        columns = edge[2 * COLS :].astype(jnp.float32)
        for i in range(ROWS + 2):
            rows = slice(i * COLS, (i + 1) * COLS)
            middle = view[1, rows].astype(jnp.float32)
            view[0, rows] = jnp.where(place == 0, columns[i : i + 1], pltpu.roll(middle, 1, 0)).astype(jnp.bfloat16)
            after = jnp.where(place == COLS - 1, columns[16 + i : 17 + i], pltpu.roll(middle, COLS - 1, 0))
            view[2, rows] = after.astype(jnp.bfloat16)

    steps = dict(
        own=own, near=near, share=share, conv=conv, swap=swap, mlp=mlp, mlp_y=mlp_y, up=up, down=down, other=other,
        share_up=share_up, share_down=share_down, embed=embed, halo=halo, frame_other=frame_other,
    )
    for name, *args in ORDER:
        steps[name](*args)

    net.wait("swap")
    mine, theirs = total[:TOKENS], got[...].astype(jnp.float32)
    convolved = jnp.concatenate([jnp.where(y_hi == 0, mine, theirs), jnp.where(y_hi == 0, theirs, mine)], axis=1)
    mixed = (embedded[...].astype(jnp.float32) + convolved + vecs[1][...]).astype(jnp.bfloat16).astype(jnp.float32)
    center = jnp.mean(mixed, axis=1, keepdims=True)
    spread = jnp.mean((mixed - center) ** 2, axis=1, keepdims=True)
    normed[...] = ((mixed - center) * lax.rsqrt(spread + 1e-05) * vecs[2][...]).astype(jnp.bfloat16)
    summed[...] = mixed + vecs[3][...]

    def wait_shared(k, s):
        net.wait(("share_up", k, s), ("share_bias", k, s), ("share_down", k, s))
        i = slot(k, s)
        bias[:, i * 4 * UNITS : (i + 1) * 4 * UNITS] = jnp.sum(bu[i].reshape(4, 8, 4 * UNITS), axis=0)

    ups, downs = wu.reshape(NZ * 4 * UNITS, WIDTH), wd.reshape(NZ * 4 * UNITS, WIDTH)

    def hidden_tiles(begin, end):
        for j in range(begin, end):
            units = slice(j * TILE, (j + 1) * TILE)
            hidden[:, units] = gelu(nt(normed[...], ups[units]) + bias[:1, units]).astype(jnp.bfloat16)
        units = slice(begin * TILE, end * TILE)
        return jnp.dot(hidden[:, units], downs[units], preferred_element_type=jnp.float32)

    for k, s in ((0, "p"), (1, "p"), (1, "m"), (2, "p"), (2, "m"), (3, "p"), (3, "m")):
        wait_shared(k, s)
    summed[...] += hidden_tiles(0, 10)
    wait_shared(4, "p")
    out_ref[...] = (summed[...] + hidden_tiles(10, 12)).astype(jnp.bfloat16)
    net.finish()


def body(patches, embed_weight, embed_bias, conv_weight, conv_bias, norm_gain, up_weight, up_bias, down_weight, down_bias):
    rows, cols, inputs = patches.shape
    bf16, f32 = jnp.bfloat16, jnp.float32
    out = pl.pallas_call(
        kernel,
        out_shape=jax.ShapeDtypeStruct((TOKENS, WIDTH), bf16),
        in_specs=[pl.BlockSpec(memory_space=pl.ANY)] * 10,
        out_specs=pl.BlockSpec(memory_space=pltpu.VMEM),
        scratch_shapes=[
            pltpu.VMEM((TAPS, NX, 2, HALF, WIDTH), bf16),
            pltpu.VMEM((NZ, 2, 2, UNITS, WIDTH), bf16),
            pltpu.VMEM((NZ, 2, 2, UNITS, WIDTH), bf16),
            pltpu.VMEM((NZ, 2, 2, 8, 4 * UNITS), f32),
            pltpu.VMEM((TOKENS, inputs), bf16),
            pltpu.VMEM((inputs, WIDTH), bf16),
            *[pltpu.VMEM((WIDTH,), f32)] * 4,
            pltpu.VMEM((1, UNITS), f32),
            pltpu.VMEM((TOKENS, WIDTH), f32),
            pltpu.VMEM((TOKENS, WIDTH), bf16),
            pltpu.VMEM((2, 3, TOKENS + 2 * COLS, WIDTH), bf16),
            pltpu.VMEM((3, ROWS, WIDTH), f32),
            pltpu.VMEM((3, ROWS, WIDTH), f32),
            pltpu.VMEM((ROWS, WIDTH), f32),
            pltpu.VMEM((ROWS, WIDTH), f32),
            pltpu.VMEM((2, 2 * COLS + 32, WIDTH), bf16),
            pltpu.VMEM((2 * TOKENS, OUT), f32),
            pltpu.VMEM((TOKENS, OUT), bf16),
            pltpu.VMEM((TOKENS, OUT), bf16),
            pltpu.VMEM((TOKENS, WIDTH), f32),
            pltpu.VMEM((TOKENS, WIDTH), bf16),
            pltpu.VMEM((TOKENS, NZ * 4 * UNITS), bf16),
            pltpu.VMEM((8, NZ * 4 * UNITS), f32),
            pltpu.SemaphoreType.DMA((10,)),
            pltpu.SemaphoreType.DMA((COPIES,)),
            pltpu.SemaphoreType.DMA((COPIES,)),
        ],
        compiler_params=pltpu.CompilerParams(collective_id=0, has_side_effects=True, vmem_limit_bytes=56 << 20),
        cost_estimate=pl.CostEstimate(flops=5_570_000_000, bytes_accessed=5_000_000, transcendentals=1_000_000),
        name="block",
    )(
        patches.reshape(TOKENS, inputs),
        embed_weight,
        jnp.swapaxes(conv_weight, 2, 3).reshape(TAPS, 2, HALF, WIDTH),
        up_weight.T,
        down_weight.T,
        embed_bias,
        conv_bias,
        norm_gain,
        up_bias,
        down_bias,
    )
    return out.reshape(rows, cols, WIDTH)


def solution(mesh):
    in_specs = (
        P("lat", "lon", None),
        P(),
        P(),
        P(None, None, None, "lat"),
        P(),
        P(),
        P(None, "lon"),
        P(None, "lon"),
        P(None, "lon"),
        P(),
    )
    return jax.shard_map(body, mesh=mesh, in_specs=in_specs, out_specs=P("lat", "lon", None), check_vma=False)
```

time: 63.8 us -> 59.5 us (0.933)
  Pallas kernels: 61.9 us -> 57.6 us
    pallas_call x1, Pallas kernels: 61.9 us -> 57.6 us  [body(): pl.pallas_call(kernel, out_shape=jax.ShapeDtypeStruct((TOKENS, WIDTH), bf...]
where the time goes in v4:
time: 59.5 us; the launch traced here: 59.4 us
  Pallas kernels  57.6 us (97%)
  local copies, waits for them, and re-layouts  1.77 us (3%)
    pallas_call x1, Pallas kernels, body(): pl.pallas_call(kernel, out_shape=jax.ShapeDtypeStruct((TOKENS, WIDTH), bf...  57.6 us
    unnamed x1, local copies, waits for them, and re-layouts  1.77 us

profile of v4, /device:TPU:1, one launch (start us, length us, event | category | flops | bytes accessed | tf_op | source)
XLA Modules:
  0.0 59.4 jit_solution(4814606339973380537)
XLA Ops:
  0.0 57.6 %block.1 = bf16[256,768]{1,0:T(8,128)(2,1)} custom-call(bf16[256,1104]{1,0:T(8,128)(2,1)} %bitcast.9, bf16[1104,768]{1,0:T(8,128)(2,1)} %embed_hbm.1, bf16[9,2,48,768]{3,2,1,0:T(8,128)(2,1)} %bitcast.8, bf16[96,768]{1,0:T(8,128)(2,1)} %bitcast.10, bf16[96,768]{1,0:T(8,128)(2,1)} %bitcast.11, f32[768]{0:T(1024)} %embed_bias_hbm.1, f32[768]{0:T(1024)} %conv_bias_hbm.1, ...), custom_call_target="tpu_custom_call" | custom-call | flops 5569999872 | bytes 5000000 | tf_op jit(solution)/shard_map/block/pallas_call | solution.py:341
  57.6 1.8 %copy.12 = bf16[8,32,768]{2,1,0:T(8,128)(2,1)} copy(bf16[8,32,768]{2,1,0:T(8,128)(2,1)} %bitcast.7) | data formatting | bytes 786432

commit v5 on v4

--- a/solution.py
+++ b/solution.py
@@ -11,22 +11,28 @@
 TOKENS, HALF, TILE = ROWS * COLS, UNITS // 2, 256
 OUT = WIDTH // 2
 TAPS = 9
-COPIES = 160
+COPIES = 240
+PARTS = ("u0", "u1", "d0", "d1")
 WAY = (1, -1, 1, -1, 1, -1, 1, -1, 1)
-Y_LINK = {"yd0": "L", "yd4": "L", "yd4m": "L", "ydm": "L", "ydp": "H", "yu0": "L", "yu4": "L", "yum": "H", "yup": "L"}
+Y_LINK = {"d00": "H", "d04": "L", "d0m": "L", "d0p": "H", "d10": "H", "d14": "L", "d1m": "L", "d1p": "H", "u10": "L", "u14": "L", "u1m": "L", "u1p": "L"}
 ORDER = (
-    ("mlp",), ("own", 5), ("own", 0), ("embed",), ("own", 1), ("own", 2), ("own", 3), ("own", 4), ("own", 6),
-    ("mlp_y",), ("near", 5), ("own", 7), ("up", 1, "p"), ("up", 1, "m"), ("share_up", 0, "p"), ("near", 0),
-    ("own", 8), ("halo",), ("near", 1), ("down", 1, "p"), ("down", 1, "m"), ("share_down", 0, "p"), ("near", 2),
-    ("other", 1, "p"), ("near", 3), ("other", 1, "m"), ("share_up", 1, "p"), ("near", 4), ("share_down", 1, "m"),
-    ("up", 2, "p"), ("up", 2, "m"), ("share_up", 1, "m"), ("near", 6), ("share", 5), ("down", 2, "p"),
-    ("down", 2, "m"), ("near", 7), ("frame_other",), ("share", 0), ("conv", 5), ("other", 2, "p"), ("other", 2, "m"),
-    ("share_up", 2, "p"), ("near", 8), ("conv", 0), ("share", 1), ("share_down", 1, "p"), ("share", 2), ("conv", 1),
-    ("share", 3), ("up", 3, "m"), ("up", 3, "p"), ("share_up", 2, "m"), ("share", 4), ("share_down", 2, "m"),
-    ("conv", 2), ("share", 7), ("conv", 3), ("share", 6), ("conv", 4), ("down", 3, "p"), ("down", 3, "m"),
-    ("share_down", 2, "p"), ("share", 8), ("conv", 6), ("conv", 7), ("other", 3, "p"), ("other", 3, "m"),
-    ("share_up", 3, "p"), ("conv", 8), ("swap",), ("share_up", 3, "m"), ("up", 4, "m"), ("share_down", 3, "p"),
-    ("share_down", 3, "m"), ("down", 4, "p"), ("down", 4, "m"), ("share_up", 4, "p"), ("share_down", 4, "p"),
+    ("own", 0), ("own", 1), ("mlp",), ("embed",), ("own", 2), ("own", 3), ("near", 0), ("mlp_y",),
+    ("pass", "u0", 1, "m"), ("pass", "u0", 1, "p"), ("own", 4), ("near", 1), ("share_up", 0, "p"),
+    ("pass", "u1", 1, "p"), ("pass", "u1", 1, "m"), ("bias_sum",), ("share_down", 0, "p"), ("halo",), ("own", 5),
+    ("pass", "d0", 1, "p"), ("pass", "d0", 1, "m"), ("near", 2), ("own", 6), ("near", 3), ("pass", "d1", 1, "p"),
+    ("pass", "d1", 1, "m"), ("own", 7), ("other", 1, "p"), ("other", 1, "m"), ("share_up", 1, "p"),
+    ("share_up", 1, "m"), ("share", 0), ("own", 8), ("share", 1), ("pass", "u0", 2, "p"), ("pass", "u0", 2, "m"),
+    ("near", 4), ("near", 5), ("pass", "u1", 2, "p"), ("pass", "u1", 2, "m"), ("bias", 1, "p"), ("bias", 1, "m"),
+    ("share_down", 1, "m"), ("pass", "d0", 2, "p"), ("pass", "d0", 2, "m"), ("share", 2), ("share", 3),
+    ("pass", "d1", 2, "p"), ("pass", "d1", 2, "m"), ("near", 6), ("frame_other",), ("conv", 0), ("other", 2, "m"),
+    ("near", 7), ("other", 2, "p"), ("share_up", 2, "p"), ("share_up", 2, "m"), ("conv", 1), ("conv", 2), ("conv", 3),
+    ("pass", "u0", 3, "p"), ("near", 8), ("share_down", 1, "p"), ("share", 5), ("share_down", 2, "m"),
+    ("pass", "u1", 3, "p"), ("pass", "u1", 3, "m"), ("bias", 2, "p"), ("bias", 2, "m"), ("share", 4), ("conv", 5),
+    ("share", 7), ("pass", "d0", 3, "p"), ("pass", "d0", 3, "m"), ("conv", 4), ("share", 6), ("share_down", 2, "p"),
+    ("conv", 7), ("pass", "d1", 3, "p"), ("pass", "d1", 3, "m"), ("share", 8), ("conv", 6), ("other", 3, "p"),
+    ("share_up", 3, "p"), ("share_up", 3, "m"), ("conv", 8), ("swap",), ("pass", "u1", 4, "m"), ("bias", 3, "m"),
+    ("share_down", 3, "p"), ("share_down", 3, "m"), ("pass", "d0", 4, "p"), ("pass", "d1", 4, "m"),
+    ("share_up", 4, "p"), ("share_down", 4, "p"),
 )
 
 
@@ -71,8 +77,8 @@
 def kernel(
     patches_hbm, embed_hbm, conv_hbm, up_hbm, down_hbm, embed_bias_hbm, conv_bias_hbm, gain_hbm, up_bias_hbm, down_bias_hbm,
     out_ref,
-    wc, wu, wd, bu, patches, we, v0, v1, v2, v3, ub, act, embedded, views, left, right, first, last, edges, total, give, got,
-    summed, normed, hidden, bias, local_sem, send_sem, recv_sem,
+    wc, wu, wd, pieces, bias, patches, we, v0, v1, v2, v3, ub, act, embedded, views, left, right, first, last, edges, total, give, got,
+    summed, normed, hidden, biases, local_sem, send_sem, recv_sem,
 ):
     vecs = (v0, v1, v2, v3)
     lon, lat = lax.axis_index("lon"), lax.axis_index("lat")
@@ -92,6 +98,7 @@
     z_links = {"p": device(x, y_hi, along_z(1), y_lo, core), "m": device(x, y_hi, along_z(-1), y_lo, core)}
     pair = device(x, 1 - y_hi, z, 1 - y_lo, core)
     across = device(x, y_hi, z, 1 - y_lo, core)
+    across_twin = device(x, y_hi, z, 1 - y_lo, 1 - core)
     y_links = {"L": across, "H": pair}
     twin = device(x, y_hi, z, y_lo, 1 - core)
 
@@ -116,7 +123,7 @@
     fetch("down", down_hbm, wd.at[0, y_lo, core])
 
     barrier = pltpu.get_barrier_semaphore()
-    partners = [*x_links.values(), *z_links.values(), pair, across, twin] + around
+    partners = [*x_links.values(), *z_links.values(), pair, across, twin, across_twin] + around
     for partner in partners:
         pl.semaphore_signal(barrier, inc=1, device_id=partner, device_id_type=MESH)
     pl.semaphore_wait(barrier, len(partners))
@@ -146,104 +153,81 @@
         a, b = t // 3, t % 3
         rows = slice(a * COLS, a * COLS + TOKENS)
         term = nt(jnp.concatenate([views[0, b, rows], views[1, b, rows]]), taps[t])
-        total[...] = term if t == 5 else total[...] + term
+        total[...] = term if t == 0 else total[...] + term
 
     def swap():
         give[...] = total[TOKENS:].astype(jnp.bfloat16)
         net.send("swap", give, got, pair)
 
+    halves = {"0": pl.ds(0, HALF), "1": pl.ds(HALF, HALF)}
+    held = {"u": wu, "d": wd}
+
+    def block(p, k, s, lo):
+        return held[p[0]].at[slot(k, s), lo, core, halves[p[1]]]
+
     def mlp():
-        near_half = pl.ds(0, HALF)
-        net.send("up_lo", up_hbm.at[near_half], wu.at[0, y_lo, core, near_half], across)
-        for s, link in z_links.items():
-            net.send(("u", 1, s), up_hbm, wu.at[slot(1, s), y_lo, core], link)
-        for s, link in z_links.items():
-            net.send(("d", 1, s), down_hbm, wd.at[slot(1, s), y_lo, core], link)
-        far_half = pl.ds(HALF, HALF)
-        net.send(("yu", 0, "p"), up_hbm.at[far_half], wu.at[0, y_lo, core, far_half], y_links[Y_LINK["yu0"]])
-        net.send(("yd", 0, "p"), down_hbm, wd.at[0, y_lo, core], y_links[Y_LINK["yd0"]])
+        given = {"u": up_hbm, "d": down_hbm}
+        net.send("up_lo", up_hbm.at[halves["0"]], block("u0", 0, "p", y_lo), across)
+        for p in PARTS:
+            for s, link in z_links.items():
+                net.send((p, 1, s), given[p[0]].at[halves[p[1]]], block(p, 1, s, y_lo), link)
+        for p in PARTS[1:]:
+            net.send(("y" + p, 0, "p"), given[p[0]].at[halves[p[1]]], block(p, 0, "p", y_lo), y_links[Y_LINK[p + "0"]])
         local.pop("up_bias").wait()
         row = jnp.concatenate([ub[...], jnp.zeros((1, 3 * UNITS), jnp.float32)], axis=1)
-        row = jnp.broadcast_to(row, (8, 4 * UNITS))
-        bu[0, y_lo, core] = pltpu.roll(row, UNITS * (2 * y_lo + core), 1)
-        piece = bu.at[0, y_lo, core]
-        net.send("bias_lo", piece, piece, across)
+        row = pltpu.roll(jnp.broadcast_to(row, (8, 4 * UNITS)), UNITS * (2 * y_lo + core), 1)
+        pieces[0] = row[:1]
+        for i, chip in enumerate((twin, across, across_twin)):
+            net.send(("piece", i), pieces.at[0], pieces.at[i + 1], chip)
+
+    def bias_sum():
+        net.wait(*(("piece", i) for i in range(3)))
+        bias[0] = pieces[0] + pieces[1] + pieces[2] + pieces[3]
         for s, link in z_links.items():
-            net.send(("bias_own", s), piece, bu.at[slot(1, s), y_lo, core], link)
+            net.send(("bias", 1, s), bias.at[0], bias.at[slot(1, s)], link)
+
+    def pass_bias(k, s):
+        net.wait(("bias", k, s))
+        net.send(("bias", k + 1, s), bias.at[slot(k, s)], bias.at[slot(k + 1, s)], z_links[s])
 
     def mlp_y():
-        net.wait("up_lo", "bias_lo")
-        half = pl.ds(0, HALF)
+        net.wait("up_lo")
         for s, link in z_links.items():
-            net.send(("v", 1, s), wu.at[0, 1 - y_lo, core, half], wu.at[slot(1, s), 1 - y_lo, core, half], link)
-            net.send(("bias_other", s), bu.at[0, 1 - y_lo, core], bu.at[slot(1, s), 1 - y_lo, core], link)
-
-    def part(k, s):
-        return pl.ds(0, UNITS) if k < 3 else pl.ds(0 if s == "p" else HALF, HALF)
-
-    def up(k, s):
-        net.wait(("u", k, s))
-        here = wu.at[slot(k, s), y_lo, core]
-        if k < 4:
-            there = wu.at[slot(k + 1, s), y_lo, core]
-            net.send(("u", k + 1, s), here.at[part(k, s)], there.at[part(k, s)], z_links[s])
-        block = here.at[pl.ds(HALF, HALF)]
-        if k < 4:
-            net.send(("yu", k, s), block, block, y_links[Y_LINK["yu" + s]])
-        else:
-            net.send(("yu", k, "p"), block, block, y_links[Y_LINK["yu4"]])
-
-    def down(k, s):
-        net.wait(("d", k, s))
-        here = wd.at[slot(k, s), y_lo, core]
-        if k < 4:
-            there = wd.at[slot(k + 1, s), y_lo, core]
-            net.send(("d", k + 1, s), here.at[part(k, s)], there.at[part(k, s)], z_links[s])
-            net.send(("yd", k, s), here, here, y_links[Y_LINK["yd" + s]])
-        else:
-            block = here.at[part(3, s)]
-            net.send(("yd", k, s), block, block, y_links[Y_LINK["yd4" if s == "p" else "yd4m"]])
-
-    def wait_other(k, s):
-        if k == 1:
-            net.wait(("v", 1, s), ("bias_own", s), ("bias_other", s))
-        elif k < 4:
-            net.wait(("v", k, s), ("bias", k, s))
-        else:
-            net.wait(("v", 4, "p"), ("bias", 4, "m"))
+            net.send(("v", 1, s), block("u0", 0, s, 1 - y_lo), block("u0", 1, s, 1 - y_lo), link)
 
     def other(k, s):
-        wait_other(k, s)
-        half = pl.ds(0, HALF)
-        if k < 3 or s == "p":
-            block, there = wu.at[slot(k, s), 1 - y_lo, core, half], wu.at[slot(k + 1, s), 1 - y_lo, core, half]
-            net.send(("v", k + 1, s), block, there, z_links[s])
-        if k < 3 or s == "m":
-            net.send(("bias", k + 1, s), bu.at[slot(k, s), :, core], bu.at[slot(k + 1, s), :, core], z_links[s])
+        net.wait(("v", k, s))
+        net.send(("v", k + 1, s), block("u0", k, s, 1 - y_lo), block("u0", k + 1, s, 1 - y_lo), z_links[s])
+
+    def pass_on(p, k, s):
+        net.wait((p, k, s))
+        here = block(p, k, s, y_lo)
+        if k < 3 or (k == 3 and (p[1] == "0") == (s == "p")):
+            net.send((p, k + 1, s), here, block(p, k + 1, s, y_lo), z_links[s])
+        if p != "u0":
+            net.send(("y" + p, k, s), here, here, y_links[Y_LINK[p + (s if k < 4 else "4")]])
 
     def share_up(k, s):
         if k == 0:
-            net.wait("up_lo", "bias_lo", ("yu", 0, "p"))
+            net.wait("up_lo", ("yu1", 0, "p"))
             local.pop("up").wait()
+        elif k == 4:
+            net.wait(("u0", 4, "p"), ("u1", 4, "m"), ("v", 4, "p"), ("yu1", 4, "m"))
         else:
-            wait_other(k, s)
-            net.wait(("u", k, s), ("yu", k, s))
-        if k == 4:
-            net.wait(("u", 4, "m"))
-        block, piece = wu.at[slot(k, s), :, core], bu.at[slot(k, s), :, core]
-        net.send(("share_up", k, s), block, block, twin)
-        net.send(("share_bias", k, s), piece, piece, twin)
+            net.wait(("u0", k, s), ("u1", k, s), ("v", k, s), ("yu1", k, s))
+        all_of_core = wu.at[slot(k, s), :, core]
+        net.send(("share_up", k, s), all_of_core, all_of_core, twin)
 
     def share_down(k, s):
-        net.wait(("yd", k, s))
         if k == 0:
+            net.wait(("yd0", 0, "p"), ("yd1", 0, "p"))
             local.pop("down").wait()
+        elif k == 4:
+            net.wait(("d0", 4, "p"), ("d1", 4, "m"), ("yd0", 4, "p"), ("yd1", 4, "m"))
         else:
-            net.wait(("d", k, s))
-        if k == 4:
-            net.wait(("d", 4, "m"), ("yd", 4, "m"))
-        block = wd.at[slot(k, s), :, core]
-        net.send(("share_down", k, s), block, block, twin)
+            net.wait(("d0", k, s), ("d1", k, s), ("yd0", k, s), ("yd1", k, s))
+        all_of_core = wd.at[slot(k, s), :, core]
+        net.send(("share_down", k, s), all_of_core, all_of_core, twin)
 
     middle_rows = pl.ds(COLS, TOKENS)
 
@@ -298,8 +282,8 @@
             view[2, rows] = after.astype(jnp.bfloat16)
 
     steps = dict(
-        own=own, near=near, share=share, conv=conv, swap=swap, mlp=mlp, mlp_y=mlp_y, up=up, down=down, other=other,
-        share_up=share_up, share_down=share_down, embed=embed, halo=halo, frame_other=frame_other,
+        own=own, near=near, share=share, conv=conv, swap=swap, mlp=mlp, mlp_y=mlp_y, **{"pass": pass_on}, other=other,
+        share_up=share_up, share_down=share_down, bias=pass_bias, bias_sum=bias_sum, embed=embed, halo=halo, frame_other=frame_other,
     )
     for name, *args in ORDER:
         steps[name](*args)
@@ -314,16 +298,16 @@
     summed[...] = mixed + vecs[3][...]
 
     def wait_shared(k, s):
-        net.wait(("share_up", k, s), ("share_bias", k, s), ("share_down", k, s))
+        net.wait(("share_up", k, s), ("share_down", k, s), *([("bias", k, "m" if k == 4 else s)] if k else []))
         i = slot(k, s)
-        bias[:, i * 4 * UNITS : (i + 1) * 4 * UNITS] = jnp.sum(bu[i].reshape(4, 8, 4 * UNITS), axis=0)
+        biases[:, i * 4 * UNITS : (i + 1) * 4 * UNITS] = bias[i]
 
     ups, downs = wu.reshape(NZ * 4 * UNITS, WIDTH), wd.reshape(NZ * 4 * UNITS, WIDTH)
 
     def hidden_tiles(begin, end):
         for j in range(begin, end):
             units = slice(j * TILE, (j + 1) * TILE)
-            hidden[:, units] = gelu(nt(normed[...], ups[units]) + bias[:1, units]).astype(jnp.bfloat16)
+            hidden[:, units] = gelu(nt(normed[...], ups[units]) + biases[:, units]).astype(jnp.bfloat16)
         units = slice(begin * TILE, end * TILE)
         return jnp.dot(hidden[:, units], downs[units], preferred_element_type=jnp.float32)
 
@@ -347,7 +331,8 @@
             pltpu.VMEM((TAPS, NX, 2, HALF, WIDTH), bf16),
             pltpu.VMEM((NZ, 2, 2, UNITS, WIDTH), bf16),
             pltpu.VMEM((NZ, 2, 2, UNITS, WIDTH), bf16),
-            pltpu.VMEM((NZ, 2, 2, 8, 4 * UNITS), f32),
+            pltpu.VMEM((4, 1, 4 * UNITS), f32),
+            pltpu.VMEM((NZ, 1, 4 * UNITS), f32),
             pltpu.VMEM((TOKENS, inputs), bf16),
             pltpu.VMEM((inputs, WIDTH), bf16),
             *[pltpu.VMEM((WIDTH,), f32)] * 4,
@@ -366,7 +351,7 @@
             pltpu.VMEM((TOKENS, WIDTH), f32),
             pltpu.VMEM((TOKENS, WIDTH), bf16),
             pltpu.VMEM((TOKENS, NZ * 4 * UNITS), bf16),
-            pltpu.VMEM((8, NZ * 4 * UNITS), f32),
+            pltpu.VMEM((1, NZ * 4 * UNITS), f32),
             pltpu.SemaphoreType.DMA((10,)),
             pltpu.SemaphoreType.DMA((COPIES,)),
             pltpu.SemaphoreType.DMA((COPIES,)),

time: 59.5 us -> 56.4 us (0.948)
  Pallas kernels: 57.6 us -> 54.5 us
    pallas_call x1, Pallas kernels: 57.6 us -> 54.5 us  [body(): pl.pallas_call(kernel, out_shape=jax.ShapeDtypeStruct((TOKENS, WIDTH), bf...]
where the time goes in v5:
time: 56.4 us; the launch traced here: 56.2 us
  Pallas kernels  54.5 us (97%)
  local copies, waits for them, and re-layouts  1.77 us (3%)
    pallas_call x1, Pallas kernels, body(): pl.pallas_call(kernel, out_shape=jax.ShapeDtypeStruct((TOKENS, WIDTH), bf...  54.5 us
    unnamed x1, local copies, waits for them, and re-layouts  1.77 us

profile of v5, /device:TPU:1, one launch (start us, length us, event | category | flops | bytes accessed | tf_op | source)
XLA Modules:
  0.0 56.2 jit_solution(11650179861212319922)
XLA Ops:
  0.0 54.5 %block.1 = bf16[256,768]{1,0:T(8,128)(2,1)} custom-call(bf16[256,1104]{1,0:T(8,128)(2,1)} %bitcast.9, bf16[1104,768]{1,0:T(8,128)(2,1)} %embed_hbm.1, bf16[9,2,48,768]{3,2,1,0:T(8,128)(2,1)} %bitcast.8, bf16[96,768]{1,0:T(8,128)(2,1)} %bitcast.10, bf16[96,768]{1,0:T(8,128)(2,1)} %bitcast.11, f32[768]{0:T(1024)} %embed_bias_hbm.1, f32[768]{0:T(1024)} %conv_bias_hbm.1, ...), custom_call_target="tpu_custom_call" | custom-call | flops 5569999872 | bytes 5000000 | tf_op jit(solution)/shard_map/block/pallas_call | solution.py:325
  54.5 1.8 %copy.12 = bf16[8,32,768]{2,1,0:T(8,128)(2,1)} copy(bf16[8,32,768]{2,1,0:T(8,128)(2,1)} %bitcast.7) | data formatting | bytes 786432

commit v6 on v5

--- a/solution.py
+++ b/solution.py
@@ -11,33 +11,30 @@
 TOKENS, HALF, TILE = ROWS * COLS, UNITS // 2, 256
 OUT = WIDTH // 2
 TAPS = 9
-COPIES = 240
-PARTS = ("u0", "u1", "d0", "d1")
+COPIES = 133
+PARTS = range(4)
+OWN, NEAR, SHARE, CONV, SWAP, MLP, MLP_Y, PASS, OTHER, SHARE_UP, SHARE_DOWN, EMBED, HALO, FRAME, BIAS, BIAS_SUM = range(16)
 WAY = (1, -1, 1, -1, 1, -1, 1, -1, 1)
-Y_LINK = {"d00": "H", "d04": "L", "d0m": "L", "d0p": "H", "d10": "H", "d14": "L", "d1m": "L", "d1p": "H", "u10": "L", "u14": "L", "u1m": "L", "u1p": "L"}
+Y_LINK = {(2, 0): 1, (2, 4): 0, (2, -1): 0, (2, 1): 1, (3, 0): 1, (3, 4): 0, (3, -1): 0, (3, 1): 1, (1, 0): 0, (1, 4): 0, (1, -1): 0, (1, 1): 0}
 ORDER = (
-    ("own", 0), ("own", 1), ("mlp",), ("embed",), ("own", 2), ("own", 3), ("near", 0), ("mlp_y",),
-    ("pass", "u0", 1, "m"), ("pass", "u0", 1, "p"), ("own", 4), ("near", 1), ("share_up", 0, "p"),
-    ("pass", "u1", 1, "p"), ("pass", "u1", 1, "m"), ("bias_sum",), ("share_down", 0, "p"), ("halo",), ("own", 5),
-    ("pass", "d0", 1, "p"), ("pass", "d0", 1, "m"), ("near", 2), ("own", 6), ("near", 3), ("pass", "d1", 1, "p"),
-    ("pass", "d1", 1, "m"), ("own", 7), ("other", 1, "p"), ("other", 1, "m"), ("share_up", 1, "p"),
-    ("share_up", 1, "m"), ("share", 0), ("own", 8), ("share", 1), ("pass", "u0", 2, "p"), ("pass", "u0", 2, "m"),
-    ("near", 4), ("near", 5), ("pass", "u1", 2, "p"), ("pass", "u1", 2, "m"), ("bias", 1, "p"), ("bias", 1, "m"),
-    ("share_down", 1, "m"), ("pass", "d0", 2, "p"), ("pass", "d0", 2, "m"), ("share", 2), ("share", 3),
-    ("pass", "d1", 2, "p"), ("pass", "d1", 2, "m"), ("near", 6), ("frame_other",), ("conv", 0), ("other", 2, "m"),
-    ("near", 7), ("other", 2, "p"), ("share_up", 2, "p"), ("share_up", 2, "m"), ("conv", 1), ("conv", 2), ("conv", 3),
-    ("pass", "u0", 3, "p"), ("near", 8), ("share_down", 1, "p"), ("share", 5), ("share_down", 2, "m"),
-    ("pass", "u1", 3, "p"), ("pass", "u1", 3, "m"), ("bias", 2, "p"), ("bias", 2, "m"), ("share", 4), ("conv", 5),
-    ("share", 7), ("pass", "d0", 3, "p"), ("pass", "d0", 3, "m"), ("conv", 4), ("share", 6), ("share_down", 2, "p"),
-    ("conv", 7), ("pass", "d1", 3, "p"), ("pass", "d1", 3, "m"), ("share", 8), ("conv", 6), ("other", 3, "p"),
-    ("share_up", 3, "p"), ("share_up", 3, "m"), ("conv", 8), ("swap",), ("pass", "u1", 4, "m"), ("bias", 3, "m"),
-    ("share_down", 3, "p"), ("share_down", 3, "m"), ("pass", "d0", 4, "p"), ("pass", "d1", 4, "m"),
-    ("share_up", 4, "p"), ("share_down", 4, "p"),
+    (OWN, 0), (OWN, 1), (MLP,), (EMBED,), (OWN, 2), (OWN, 3), (NEAR, 0), (MLP_Y,), (PASS, 0, 1, -1), (PASS, 0, 1, 1),
+    (OWN, 4), (NEAR, 1), (SHARE_UP, 0, 1), (PASS, 1, 1, 1), (PASS, 1, 1, -1), (BIAS_SUM,), (SHARE_DOWN, 0, 1),
+    (HALO,), (OWN, 5), (PASS, 2, 1, 1), (PASS, 2, 1, -1), (NEAR, 2), (OWN, 6), (NEAR, 3), (PASS, 3, 1, 1),
+    (PASS, 3, 1, -1), (OWN, 7), (OTHER, 1, 1), (OTHER, 1, -1), (SHARE_UP, 1, 1), (SHARE_UP, 1, -1), (SHARE, 0),
+    (OWN, 8), (SHARE, 1), (PASS, 0, 2, 1), (PASS, 0, 2, -1), (NEAR, 4), (NEAR, 5), (PASS, 1, 2, 1), (PASS, 1, 2, -1),
+    (BIAS, 1, 1), (BIAS, 1, -1), (SHARE_DOWN, 1, -1), (PASS, 2, 2, 1), (PASS, 2, 2, -1), (SHARE, 2), (SHARE, 3),
+    (PASS, 3, 2, 1), (PASS, 3, 2, -1), (NEAR, 6), (FRAME,), (CONV, 0), (OTHER, 2, -1), (NEAR, 7), (OTHER, 2, 1),
+    (SHARE_UP, 2, 1), (SHARE_UP, 2, -1), (CONV, 1), (CONV, 2), (CONV, 3), (PASS, 0, 3, 1), (NEAR, 8),
+    (SHARE_DOWN, 1, 1), (SHARE, 5), (SHARE_DOWN, 2, -1), (PASS, 1, 3, 1), (PASS, 1, 3, -1), (BIAS, 2, 1),
+    (BIAS, 2, -1), (SHARE, 4), (CONV, 5), (SHARE, 7), (PASS, 2, 3, 1), (PASS, 2, 3, -1), (CONV, 4), (SHARE, 6),
+    (SHARE_DOWN, 2, 1), (CONV, 7), (PASS, 3, 3, 1), (PASS, 3, 3, -1), (SHARE, 8), (CONV, 6), (OTHER, 3, 1),
+    (SHARE_UP, 3, 1), (SHARE_UP, 3, -1), (CONV, 8), (SWAP,), (PASS, 1, 4, -1), (BIAS, 3, -1), (SHARE_DOWN, 3, 1),
+    (SHARE_DOWN, 3, -1), (PASS, 2, 4, 1), (PASS, 3, 4, -1), (SHARE_UP, 4, 1), (SHARE_DOWN, 4, 1),
 )
 
 
 def slot(k, s):
-    return 7 if k == 4 else 0 if k == 0 else 2 * k - (s == "p")
+    return 7 if k == 4 else 0 if k == 0 else 2 * k - (s == 1)
 
 
 def gelu(v):
@@ -56,7 +53,7 @@
     def send(self, name, src, dst, device):
         i = len(self.made)
         copy = pltpu.make_async_remote_copy(
-            src_ref=src, dst_ref=dst, send_sem=self.send_sem.at[i], recv_sem=self.recv_sem.at[i],
+            src_ref=src, dst_ref=dst, send_sem=self.send_sem.at[0], recv_sem=self.recv_sem.at[i],
             device_id=device, device_id_type=MESH,
         )
         copy.start()
@@ -71,6 +68,7 @@
     def finish(self):
         for name, copy in self.made.items():
             self.wait(name)
+        for copy in self.made.values():
             copy.wait_send()
 
 
@@ -95,11 +93,11 @@
         return (z + d + NZ) % NZ
 
     x_links = {1: device(along_x(1), y_hi, z, y_lo, core), -1: device(along_x(-1), y_hi, z, y_lo, core)}
-    z_links = {"p": device(x, y_hi, along_z(1), y_lo, core), "m": device(x, y_hi, along_z(-1), y_lo, core)}
+    z_links = {1: device(x, y_hi, along_z(1), y_lo, core), -1: device(x, y_hi, along_z(-1), y_lo, core)}
     pair = device(x, 1 - y_hi, z, 1 - y_lo, core)
     across = device(x, y_hi, z, 1 - y_lo, core)
     across_twin = device(x, y_hi, z, 1 - y_lo, 1 - core)
-    y_links = {"L": across, "H": pair}
+    y_links = (across, pair)
     twin = device(x, y_hi, z, y_lo, 1 - core)
 
     def token(dlat, dlon):
@@ -159,20 +157,20 @@
         give[...] = total[TOKENS:].astype(jnp.bfloat16)
         net.send("swap", give, got, pair)
 
-    halves = {"0": pl.ds(0, HALF), "1": pl.ds(HALF, HALF)}
-    held = {"u": wu, "d": wd}
+    def half(array, p):
+        return array.at[pl.ds(p % 2 * HALF, HALF)]
 
     def block(p, k, s, lo):
-        return held[p[0]].at[slot(k, s), lo, core, halves[p[1]]]
+        return half((wu if p < 2 else wd).at[slot(k, s), lo, core], p)
 
     def mlp():
-        given = {"u": up_hbm, "d": down_hbm}
-        net.send("up_lo", up_hbm.at[halves["0"]], block("u0", 0, "p", y_lo), across)
+        given = (up_hbm, up_hbm, down_hbm, down_hbm)
+        net.send("up_lo", half(up_hbm, 0), block(0, 0, 1, y_lo), across)
         for p in PARTS:
             for s, link in z_links.items():
-                net.send((p, 1, s), given[p[0]].at[halves[p[1]]], block(p, 1, s, y_lo), link)
+                net.send((p, 1, s), half(given[p], p), block(p, 1, s, y_lo), link)
         for p in PARTS[1:]:
-            net.send(("y" + p, 0, "p"), given[p[0]].at[halves[p[1]]], block(p, 0, "p", y_lo), y_links[Y_LINK[p + "0"]])
+            net.send(("y", p, 0, 1), half(given[p], p), block(p, 0, 1, y_lo), y_links[Y_LINK[p, 0]])
         local.pop("up_bias").wait()
         row = jnp.concatenate([ub[...], jnp.zeros((1, 3 * UNITS), jnp.float32)], axis=1)
         row = pltpu.roll(jnp.broadcast_to(row, (8, 4 * UNITS)), UNITS * (2 * y_lo + core), 1)
@@ -193,39 +191,39 @@
     def mlp_y():
         net.wait("up_lo")
         for s, link in z_links.items():
-            net.send(("v", 1, s), block("u0", 0, s, 1 - y_lo), block("u0", 1, s, 1 - y_lo), link)
+            net.send(("v", 1, s), block(0, 0, s, 1 - y_lo), block(0, 1, s, 1 - y_lo), link)
 
     def other(k, s):
         net.wait(("v", k, s))
-        net.send(("v", k + 1, s), block("u0", k, s, 1 - y_lo), block("u0", k + 1, s, 1 - y_lo), z_links[s])
+        net.send(("v", k + 1, s), block(0, k, s, 1 - y_lo), block(0, k + 1, s, 1 - y_lo), z_links[s])
 
     def pass_on(p, k, s):
         net.wait((p, k, s))
         here = block(p, k, s, y_lo)
-        if k < 3 or (k == 3 and (p[1] == "0") == (s == "p")):
+        if k < 3 or (k == 3 and (p % 2 == 0) == (s == 1)):
             net.send((p, k + 1, s), here, block(p, k + 1, s, y_lo), z_links[s])
-        if p != "u0":
-            net.send(("y" + p, k, s), here, here, y_links[Y_LINK[p + (s if k < 4 else "4")]])
+        if p:
+            net.send(("y", p, k, s), here, here, y_links[Y_LINK[p, s if k < 4 else 4]])
 
     def share_up(k, s):
         if k == 0:
-            net.wait("up_lo", ("yu1", 0, "p"))
+            net.wait("up_lo", ("y", 1, 0, 1))
             local.pop("up").wait()
         elif k == 4:
-            net.wait(("u0", 4, "p"), ("u1", 4, "m"), ("v", 4, "p"), ("yu1", 4, "m"))
+            net.wait((0, 4, 1), (1, 4, -1), ("v", 4, 1), ("y", 1, 4, -1))
         else:
-            net.wait(("u0", k, s), ("u1", k, s), ("v", k, s), ("yu1", k, s))
+            net.wait((0, k, s), (1, k, s), ("v", k, s), ("y", 1, k, s))
         all_of_core = wu.at[slot(k, s), :, core]
         net.send(("share_up", k, s), all_of_core, all_of_core, twin)
 
     def share_down(k, s):
         if k == 0:
-            net.wait(("yd0", 0, "p"), ("yd1", 0, "p"))
+            net.wait(("y", 2, 0, 1), ("y", 3, 0, 1))
             local.pop("down").wait()
         elif k == 4:
-            net.wait(("d0", 4, "p"), ("d1", 4, "m"), ("yd0", 4, "p"), ("yd1", 4, "m"))
+            net.wait((2, 4, 1), (3, 4, -1), ("y", 2, 4, 1), ("y", 3, 4, -1))
         else:
-            net.wait(("d0", k, s), ("d1", k, s), ("yd0", k, s), ("yd1", k, s))
+            net.wait((2, k, s), (3, k, s), ("y", 2, k, s), ("y", 3, k, s))
         all_of_core = wd.at[slot(k, s), :, core]
         net.send(("share_down", k, s), all_of_core, all_of_core, twin)
 
@@ -281,12 +279,11 @@
             after = jnp.where(place == COLS - 1, columns[16 + i : 17 + i], pltpu.roll(middle, COLS - 1, 0))
             view[2, rows] = after.astype(jnp.bfloat16)
 
-    steps = dict(
-        own=own, near=near, share=share, conv=conv, swap=swap, mlp=mlp, mlp_y=mlp_y, **{"pass": pass_on}, other=other,
-        share_up=share_up, share_down=share_down, bias=pass_bias, bias_sum=bias_sum, embed=embed, halo=halo, frame_other=frame_other,
+    steps = (
+        own, near, share, conv, swap, mlp, mlp_y, pass_on, other, share_up, share_down, embed, halo, frame_other, pass_bias, bias_sum,
     )
-    for name, *args in ORDER:
-        steps[name](*args)
+    for step, *args in ORDER:
+        steps[step](*args)
 
     net.wait("swap")
     mine, theirs = total[:TOKENS], got[...].astype(jnp.float32)
@@ -298,7 +295,7 @@
     summed[...] = mixed + vecs[3][...]
 
     def wait_shared(k, s):
-        net.wait(("share_up", k, s), ("share_down", k, s), *([("bias", k, "m" if k == 4 else s)] if k else []))
+        net.wait(("share_up", k, s), ("share_down", k, s), *([("bias", k, -1 if k == 4 else s)] if k else []))
         i = slot(k, s)
         biases[:, i * 4 * UNITS : (i + 1) * 4 * UNITS] = bias[i]
 
@@ -311,12 +308,13 @@
         units = slice(begin * TILE, end * TILE)
         return jnp.dot(hidden[:, units], downs[units], preferred_element_type=jnp.float32)
 
-    for k, s in ((0, "p"), (1, "p"), (1, "m"), (2, "p"), (2, "m"), (3, "p"), (3, "m")):
+    for k, s in ((0, 1), (1, 1), (1, -1), (2, 1), (2, -1), (3, 1), (3, -1)):
         wait_shared(k, s)
     summed[...] += hidden_tiles(0, 10)
-    wait_shared(4, "p")
+    wait_shared(4, 1)
     out_ref[...] = (summed[...] + hidden_tiles(10, 12)).astype(jnp.bfloat16)
     net.finish()
+    assert len(net.made) == COPIES
 
 
 def body(patches, embed_weight, embed_bias, conv_weight, conv_bias, norm_gain, up_weight, up_bias, down_weight, down_bias):
@@ -353,7 +351,7 @@
             pltpu.VMEM((TOKENS, NZ * 4 * UNITS), bf16),
             pltpu.VMEM((1, NZ * 4 * UNITS), f32),
             pltpu.SemaphoreType.DMA((10,)),
-            pltpu.SemaphoreType.DMA((COPIES,)),
+            pltpu.SemaphoreType.DMA((1,)),
             pltpu.SemaphoreType.DMA((COPIES,)),
         ],
         compiler_params=pltpu.CompilerParams(collective_id=0, has_side_effects=True, vmem_limit_bytes=56 << 20),

time: 56.4 us -> 53.1 us (0.941)
  Pallas kernels: 54.5 us -> 51.2 us
    pallas_call x1, Pallas kernels: 54.5 us -> 51.2 us  [body(): pl.pallas_call(kernel, out_shape=jax.ShapeDtypeStruct((TOKENS, WIDTH), bf...]
where the time goes in v6:
time: 53.1 us; the launch traced here: 52.9 us
  Pallas kernels  51.2 us (96%)
  local copies, waits for them, and re-layouts  1.77 us (3%)
    pallas_call x1, Pallas kernels, body(): pl.pallas_call(kernel, out_shape=jax.ShapeDtypeStruct((TOKENS, WIDTH), bf...  51.2 us
    unnamed x1, local copies, waits for them, and re-layouts  1.77 us

profile of v6, /device:TPU:1, one launch (start us, length us, event | category | flops | bytes accessed | tf_op | source)
XLA Modules:
  0.0 52.9 jit_solution(2821658007825316393)
XLA Ops:
  0.0 51.2 %block.1 = bf16[256,768]{1,0:T(8,128)(2,1)} custom-call(bf16[256,1104]{1,0:T(8,128)(2,1)} %bitcast.9, bf16[1104,768]{1,0:T(8,128)(2,1)} %embed_hbm.1, bf16[9,2,48,768]{3,2,1,0:T(8,128)(2,1)} %bitcast.8, bf16[96,768]{1,0:T(8,128)(2,1)} %bitcast.10, bf16[96,768]{1,0:T(8,128)(2,1)} %bitcast.11, f32[768]{0:T(1024)} %embed_bias_hbm.1, f32[768]{0:T(1024)} %conv_bias_hbm.1, ...), custom_call_target="tpu_custom_call" | custom-call | flops 5569999872 | bytes 5000000 | tf_op jit(solution)/shard_map/block/pallas_call | solution.py:323
  51.2 1.8 %copy.12 = bf16[8,32,768]{2,1,0:T(8,128)(2,1)} copy(bf16[8,32,768]{2,1,0:T(8,128)(2,1)} %bitcast.7) | data formatting | bytes 786432

commit v7 on v6

--- a/solution.py
+++ b/solution.py
@@ -15,21 +15,21 @@
 PARTS = range(4)
 OWN, NEAR, SHARE, CONV, SWAP, MLP, MLP_Y, PASS, OTHER, SHARE_UP, SHARE_DOWN, EMBED, HALO, FRAME, BIAS, BIAS_SUM = range(16)
 WAY = (1, -1, 1, -1, 1, -1, 1, -1, 1)
-Y_LINK = {(2, 0): 1, (2, 4): 0, (2, -1): 0, (2, 1): 1, (3, 0): 1, (3, 4): 0, (3, -1): 0, (3, 1): 1, (1, 0): 0, (1, 4): 0, (1, -1): 0, (1, 1): 0}
+Y_LINK = {(2, 0): 0, (2, 4): 0, (2, -1): 1, (2, 1): 0, (3, 0): 0, (3, 4): 0, (3, -1): 0, (3, 1): 1, (1, 0): 1, (1, 4): 0, (1, -1): 0, (1, 1): 0}
 ORDER = (
-    (OWN, 0), (OWN, 1), (MLP,), (EMBED,), (OWN, 2), (OWN, 3), (NEAR, 0), (MLP_Y,), (PASS, 0, 1, -1), (PASS, 0, 1, 1),
-    (OWN, 4), (NEAR, 1), (SHARE_UP, 0, 1), (PASS, 1, 1, 1), (PASS, 1, 1, -1), (BIAS_SUM,), (SHARE_DOWN, 0, 1),
-    (HALO,), (OWN, 5), (PASS, 2, 1, 1), (PASS, 2, 1, -1), (NEAR, 2), (OWN, 6), (NEAR, 3), (PASS, 3, 1, 1),
-    (PASS, 3, 1, -1), (OWN, 7), (OTHER, 1, 1), (OTHER, 1, -1), (SHARE_UP, 1, 1), (SHARE_UP, 1, -1), (SHARE, 0),
-    (OWN, 8), (SHARE, 1), (PASS, 0, 2, 1), (PASS, 0, 2, -1), (NEAR, 4), (NEAR, 5), (PASS, 1, 2, 1), (PASS, 1, 2, -1),
-    (BIAS, 1, 1), (BIAS, 1, -1), (SHARE_DOWN, 1, -1), (PASS, 2, 2, 1), (PASS, 2, 2, -1), (SHARE, 2), (SHARE, 3),
-    (PASS, 3, 2, 1), (PASS, 3, 2, -1), (NEAR, 6), (FRAME,), (CONV, 0), (OTHER, 2, -1), (NEAR, 7), (OTHER, 2, 1),
-    (SHARE_UP, 2, 1), (SHARE_UP, 2, -1), (CONV, 1), (CONV, 2), (CONV, 3), (PASS, 0, 3, 1), (NEAR, 8),
-    (SHARE_DOWN, 1, 1), (SHARE, 5), (SHARE_DOWN, 2, -1), (PASS, 1, 3, 1), (PASS, 1, 3, -1), (BIAS, 2, 1),
-    (BIAS, 2, -1), (SHARE, 4), (CONV, 5), (SHARE, 7), (PASS, 2, 3, 1), (PASS, 2, 3, -1), (CONV, 4), (SHARE, 6),
-    (SHARE_DOWN, 2, 1), (CONV, 7), (PASS, 3, 3, 1), (PASS, 3, 3, -1), (SHARE, 8), (CONV, 6), (OTHER, 3, 1),
-    (SHARE_UP, 3, 1), (SHARE_UP, 3, -1), (CONV, 8), (SWAP,), (PASS, 1, 4, -1), (BIAS, 3, -1), (SHARE_DOWN, 3, 1),
-    (SHARE_DOWN, 3, -1), (PASS, 2, 4, 1), (PASS, 3, 4, -1), (SHARE_UP, 4, 1), (SHARE_DOWN, 4, 1),
+    (OWN, 0), (OWN, 1), (MLP,), (EMBED,), (OWN, 2), (OWN, 3), (NEAR, 0), (MLP_Y,), (PASS, 0, 1, 1), (PASS, 0, 1, -1),
+    (SHARE_UP, 0, 1), (OWN, 4), (NEAR, 1), (PASS, 1, 1, 1), (PASS, 1, 1, -1), (HALO,), (OWN, 5), (SHARE_DOWN, 0, 1),
+    (PASS, 2, 1, 1), (PASS, 2, 1, -1), (BIAS_SUM,), (NEAR, 2), (OWN, 6), (NEAR, 3), (PASS, 3, 1, 1), (PASS, 3, 1, -1),
+    (OWN, 7), (OTHER, 1, 1), (OTHER, 1, -1), (SHARE_UP, 1, 1), (SHARE_UP, 1, -1), (SHARE, 0), (OWN, 8), (SHARE, 1),
+    (PASS, 0, 2, 1), (PASS, 0, 2, -1), (NEAR, 4), (NEAR, 5), (PASS, 1, 2, 1), (PASS, 1, 2, -1), (PASS, 2, 2, 1),
+    (PASS, 2, 2, -1), (BIAS, 1, 1), (BIAS, 1, -1), (FRAME,), (SHARE, 2), (CONV, 0), (PASS, 3, 2, 1), (PASS, 3, 2, -1),
+    (SHARE, 3), (CONV, 1), (NEAR, 6), (SHARE_DOWN, 1, -1), (CONV, 2), (NEAR, 7), (OTHER, 2, 1), (OTHER, 2, -1),
+    (SHARE_UP, 2, -1), (SHARE_UP, 2, 1), (CONV, 3), (SHARE_DOWN, 1, 1), (PASS, 0, 3, 1), (NEAR, 8), (SHARE, 5),
+    (SHARE_DOWN, 2, -1), (PASS, 1, 3, 1), (PASS, 1, 3, -1), (SHARE_DOWN, 2, 1), (SHARE, 4), (CONV, 5),
+    (PASS, 2, 3, 1), (BIAS, 2, 1), (PASS, 2, 3, -1), (BIAS, 2, -1), (SHARE, 7), (SHARE, 6), (CONV, 4),
+    (PASS, 3, 3, 1), (PASS, 3, 3, -1), (CONV, 7), (SHARE, 8), (CONV, 6), (OTHER, 3, 1), (SHARE_UP, 3, 1),
+    (SHARE_UP, 3, -1), (CONV, 8), (SWAP,), (PASS, 1, 4, -1), (SHARE_DOWN, 3, 1), (BIAS, 3, -1), (SHARE_DOWN, 3, -1),
+    (PASS, 2, 4, 1), (PASS, 3, 4, -1), (SHARE_UP, 4, 1), (SHARE_DOWN, 4, 1),
 )
 
 
@@ -76,7 +76,7 @@
     patches_hbm, embed_hbm, conv_hbm, up_hbm, down_hbm, embed_bias_hbm, conv_bias_hbm, gain_hbm, up_bias_hbm, down_bias_hbm,
     out_ref,
     wc, wu, wd, pieces, bias, patches, we, v0, v1, v2, v3, ub, act, embedded, views, left, right, first, last, edges, total, give, got,
-    summed, normed, hidden, biases, local_sem, send_sem, recv_sem,
+    summed, normed, hidden, biases, done, local_sem, send_sem, recv_sem,
 ):
     vecs = (v0, v1, v2, v3)
     lon, lat = lax.axis_index("lon"), lax.axis_index("lat")
@@ -312,8 +312,19 @@
         wait_shared(k, s)
     summed[...] += hidden_tiles(0, 10)
     wait_shared(4, 1)
-    out_ref[...] = (summed[...] + hidden_tiles(10, 12)).astype(jnp.bfloat16)
+    for j in (10, 11):
+        units = slice(j * TILE, (j + 1) * TILE)
+        hidden[:, units] = gelu(nt(normed[...], ups[units]) + biases[:, units]).astype(jnp.bfloat16)
+    results = []
+    for i in range(2):
+        rows, units = pl.ds(i * TOKENS // 2, TOKENS // 2), slice(10 * TILE, 12 * TILE)
+        last_term = jnp.dot(hidden[rows, units], downs[units], preferred_element_type=jnp.float32)
+        done[rows] = (summed[rows] + last_term).astype(jnp.bfloat16)
+        results.append(pltpu.make_async_copy(done.at[rows], out_ref.at[rows], local_sem.at[i]))
+        results[i].start()
     net.finish()
+    for result in results:
+        result.wait()
     assert len(net.made) == COPIES
 
 
@@ -324,7 +335,7 @@
         kernel,
         out_shape=jax.ShapeDtypeStruct((TOKENS, WIDTH), bf16),
         in_specs=[pl.BlockSpec(memory_space=pl.ANY)] * 10,
-        out_specs=pl.BlockSpec(memory_space=pltpu.VMEM),
+        out_specs=pl.BlockSpec(memory_space=pl.ANY),
         scratch_shapes=[
             pltpu.VMEM((TAPS, NX, 2, HALF, WIDTH), bf16),
             pltpu.VMEM((NZ, 2, 2, UNITS, WIDTH), bf16),
@@ -350,6 +361,7 @@
             pltpu.VMEM((TOKENS, WIDTH), bf16),
             pltpu.VMEM((TOKENS, NZ * 4 * UNITS), bf16),
             pltpu.VMEM((1, NZ * 4 * UNITS), f32),
+            pltpu.VMEM((TOKENS, WIDTH), bf16),
             pltpu.SemaphoreType.DMA((10,)),
             pltpu.SemaphoreType.DMA((1,)),
             pltpu.SemaphoreType.DMA((COPIES,)),

time: 53.1 us -> 53 us (level)
  no operation moved by 1% of the time
where the time goes in v7:
time: 53 us; the launch traced here: 52.9 us
  Pallas kernels  51.1 us (96%)
  local copies, waits for them, and re-layouts  1.77 us (3%)
    pallas_call x1, Pallas kernels, body(): pl.pallas_call(kernel, out_shape=jax.ShapeDtypeStruct((TOKENS, WIDTH), bf...  51.1 us
    unnamed x1, local copies, waits for them, and re-layouts  1.77 us

profile of v7, /device:TPU:1, one launch (start us, length us, event | category | flops | bytes accessed | tf_op | source)
XLA Modules:
  0.0 52.9 jit_solution(2760295129512048336)
XLA Ops:
  0.0 51.1 %block.1 = bf16[256,768]{1,0:T(8,128)(2,1)} custom-call(bf16[256,1104]{1,0:T(8,128)(2,1)} %bitcast.9, bf16[1104,768]{1,0:T(8,128)(2,1)} %embed_hbm.1, bf16[9,2,48,768]{3,2,1,0:T(8,128)(2,1)} %bitcast.8, bf16[96,768]{1,0:T(8,128)(2,1)} %bitcast.10, bf16[96,768]{1,0:T(8,128)(2,1)} %bitcast.11, f32[768]{0:T(1024)} %embed_bias_hbm.1, f32[768]{0:T(1024)} %conv_bias_hbm.1, ...), custom_call_target="tpu_custom_call" | custom-call | flops 5569999872 | bytes 5000000 | tf_op jit(solution)/shard_map/block/pallas_call | solution.py:334
  51.2 1.8 %copy.12 = bf16[8,32,768]{2,1,0:T(8,128)(2,1)} copy(bf16[8,32,768]{2,1,0:T(8,128)(2,1)} %bitcast.7) | data formatting | bytes 786432
